TPU v7x, 32 devices: a whole 2x2x4 slice. The times are simulated.
32 devices in a mesh: req: 8 (over z, x), tok: 4 (over y, core).
Axes of the slice: x: 2, y: 2, z: 4, core: 2. Of those that a mesh axis runs over, the one named last changes fastest.
Arguments:
- queries: bfloat16 [4096, 2048], P('req', 'tok'), may hold values from -6 to 6
- suffix_kv: bfloat16 [4096, 2048], P('req'), may hold values from -6 to 6
- prefix_cache: bfloat16 [4096, 2048], P('req'), may hold values from -24 to 24
- q_gain: float32 [256], replicated, may hold values from 0.1 to 1.9
- k_gain: float32 [256], replicated, may hold values from 0.1 to 1.9
- lengths: int32 [8, 3], P('req'), may hold values from 1 to 256, 512 in all within a row
- group_of: int32 [8], replicated, may hold values from 0 to 1
- owner_order: int32 [8], replicated, may hold values from 0 to 7, each once
- residual: bfloat16 [4096, 2560], P('req'), may hold values from -6 to 6
- w_out: bfloat16 [2048, 2560], P('tok'), may hold values from -0.125 to 0.125
- attn_gain: float32 [2560], replicated, may hold values from 0.1 to 1.9
- ffn_in_gain: float32 [2560], replicated, may hold values from 0.1 to 1.9
- ffn_out_gain: float32 [2560], replicated, may hold values from 0.1 to 1.9
- w_gate: bfloat16 [2560, 10240], P(None, 'tok'), may hold values from -0.125 to 0.125
- w_up: bfloat16 [2560, 10240], P(None, 'tok'), may hold values from -0.125 to 0.125
- w_down: bfloat16 [10240, 2560], P('tok'), may hold values from -0.0625 to 0.0625
Outputs:
- layer_out: bfloat16 [4096, 2560], P(('req', 'tok'))
Inputs may be any that keep to these rules, and one draw needn't show every extreme that they name: The 3 lengths of each req index sum to 512; the largest is exactly 256. `owner_order`: each req index appears once; entries g * 4 to g * 4 + 3 name the holders of group g's prefix.
All inputs are finite; a program needn't handle non-finite values.
Results may differ from a plain program's by a relative error of at most 0.02.
Values may be sent and summed in bfloat16 or wider, within the bound.
No kernel may reach another device: no remote copies, remote signals or barrier semaphores. Data moves between devices by JAX's collectives and lax.ppermute only.
A program may use at most 128 MiB of HBM per device.

v0:
```python
import functools

import jax
import jax.numpy as jnp
from jax import lax
from jax.experimental import pallas as pl
from jax.experimental.pallas import tpu as pltpu
from jax.sharding import PartitionSpec as P

H = 8
KVH = 4
HD = 256
GROUPS = 2
EPSILON = 1e-06
MASKED = -1e30
CORES = 2
LINE = 4
NUMBERS = 3
FEED_LIMIT = 25
BF16 = jnp.bfloat16
F32 = jnp.float32
ANY = pl.BlockSpec(memory_space=pl.ANY)
VMEM = pl.BlockSpec(memory_space=pltpu.VMEM)
SMEM = pl.BlockSpec(memory_space=pltpu.SMEM)
HBM = pl.BlockSpec(memory_space=pltpu.HBM)


def mib(count):
    return count << 20


def in_vmem(values_in):
    return pltpu.with_memory_space_constraint(values_in, pltpu.VMEM)


def in_hbm(values_in):
    return pltpu.with_memory_space_constraint(values_in, pltpu.HBM)


def rms(values_in):
    return values_in * lax.rsqrt(jnp.mean(values_in * values_in, axis=-1, keepdims=True) + EPSILON)


def attend(query_ref, state, head, rows, keys, values, visible):
    max_ref, sum_ref, acc_ref = state
    columns = slice(head * HD, (head + 1) * HD)
    scores = lax.dot_general(
        query_ref[rows, columns], keys, (((1,), (1,)), ((), ())), preferred_element_type=F32
    )
    if visible is not None:
        scores = jnp.where(visible, scores, MASKED)
        block_max = jnp.max(scores, axis=1, keepdims=True)
        weights = jnp.exp(scores - block_max)
        max_ref[head, rows, :] = jnp.broadcast_to(block_max, (scores.shape[0], 128))
        sum_ref[head, rows, :] = jnp.broadcast_to(
            jnp.sum(weights, axis=1, keepdims=True), (scores.shape[0], 128)
        )
        acc_ref[rows, columns] = jnp.dot(weights.astype(BF16), values, preferred_element_type=F32)
        return
    old_max = max_ref[head, rows, :]
    new_max = jnp.maximum(old_max, jnp.max(scores, axis=1, keepdims=True))
    scale = jnp.exp(old_max - new_max)
    weights = jnp.exp(scores - new_max[:, :1])
    max_ref[head, rows, :] = new_max
    sum_ref[head, rows, :] = sum_ref[head, rows, :] * scale + jnp.sum(weights, axis=1, keepdims=True)
    acc_ref[rows, columns] = acc_ref[rows, columns] * scale[:, :1] + jnp.dot(
        weights.astype(BF16), values, preferred_element_type=F32
    )


def block_wanted(numbers, place, across, req_count):
    source_lines, col_shift = place
    per_group = req_count // GROUPS
    req_index = numbers[0]
    line = req_index // across
    source_line = jnp.int32(-1)
    for at, source in enumerate(source_lines):
        if source >= 0:
            source_line = jnp.where(line == at, source, source_line)
    source = source_line * across + lax.rem(lax.rem(req_index, across) + across - col_shift, across)
    holder = jnp.int32(-1)
    for slot in range(req_count):
        holder = jnp.where(numbers[NUMBERS + req_count + slot] == source, slot // per_group, holder)
    return (source_line >= 0) & (holder == numbers[NUMBERS + req_index])


def attention_kernel(places, counts, across, req_count, heads, first, parts, near, *refs):
    refs = list(refs)
    take = lambda count: [refs.pop(0) for _ in range(count)]
    (numbers,) = take(1)
    if first:
        queries_ref, suffix, gains = take(3)
    else:
        query_ref, max_in, sum_in, acc_in = take(4)
    blocks = [take(count) for count in counts]
    take(near)
    if first:
        query_ref, max_ref, sum_ref, acc_ref, queries, own_keys, own_values, held, sems, own_sems = refs
    elif parts:
        out_refs = take(parts)
        max_ref, sum_ref, acc_ref, held, sems = refs
    else:
        max_ref, sum_ref, acc_ref = take(3)
        held, sems = refs
    state = (max_ref, sum_ref, acc_ref)
    wanted = [block_wanted(numbers, place, across, req_count) for place in places]

    def copies_of(at):
        extent = held.shape[1] // counts[at]
        return [
            pltpu.make_async_copy(
                block, held.at[at, pl.ds(piece * extent, extent)], sems.at[at, piece]
            )
            for piece, block in enumerate(blocks[at])
        ]

    for at in range(len(places)):

        @pl.when(wanted[at])
        def _():
            for copy in copies_of(at):
                copy.start()

    row_count = query_ref.shape[0]
    step = min(256, row_count)
    if first:
        begin = pl.multiple_of(numbers[2] * HD, HD)
        copies = [pltpu.make_async_copy(queries_ref, queries, own_sems.at[2])] + [
            pltpu.make_async_copy(
                suffix.at[:, pl.ds(pl.multiple_of(begin + which * KVH * HD, HD), HD)],
                target,
                own_sems.at[which],
            )
            for which, target in enumerate((own_keys, own_values))
        ]
        for copy in copies:
            copy.start()
        copies[0].wait()
        for head in range(heads):
            columns = slice(head * HD, (head + 1) * HD)
            normed = (rms(queries[:, columns].astype(F32)) * gains[:1, :]).astype(BF16)
            query_ref[:, columns] = normed * jnp.asarray(HD ** (-0.5), BF16)
        for copy in copies[1:]:
            copy.wait()
        own_keys[...] = (rms(own_keys[...].astype(F32)) * gains[1:, :]).astype(BF16)
        ends = []
        first_length = NUMBERS + 2 * req_count
        for at in range(first_length, numbers.shape[0] - 1):
            ends.append(numbers[at] + (ends[-1] if ends else 0))
        for begin in range(0, row_count, step):
            rows = slice(begin, begin + step)
            seen = begin + step
            row_at = lax.broadcasted_iota(jnp.int32, (step, seen), 0) + begin
            key_at = lax.broadcasted_iota(jnp.int32, (step, seen), 1)
            visible = key_at <= row_at
            for end in ends:
                visible &= (row_at < end) | (key_at >= end)
            for head in range(heads):
                attend(query_ref, state, head, rows, own_keys[:seen, :], own_values[:seen, :], visible)
    else:
        max_ref[...] = max_in[...]
        sum_ref[...] = sum_in[...]
        acc_ref[...] = acc_in[...]

    for at in range(len(places)):

        @pl.when(wanted[at])
        def _():
            for copy in copies_of(at):
                copy.wait()

            @pl.loop(0, row_count // step)
            def _(turn):
                rows = pl.ds(pl.multiple_of(turn * step, step), step)
                for head in range(heads):
                    attend(query_ref, state, head, rows, held[at, :, :HD], held[at, :, HD:], None)


    for at in range(parts):
        extent = row_count // parts
        begin = lax.rem(numbers[1] // CORES + at, parts) * extent
        rows = pl.ds(pl.multiple_of(begin, extent), extent)
        for head in range(heads):
            columns = slice(head * HD, (head + 1) * HD)
            out_refs[at][:, columns] = (acc_ref[rows, columns] / sum_ref[head, rows, :1]).astype(BF16)


def attention_call(numbers, across, req_count, opening, state, wave, parts, near=()):
    blocks = [block for parts_of, _, _ in wave for block in parts_of]
    counts = [len(parts_of) for parts_of, _, _ in wave]
    places = [(sources, shift) for _, sources, shift in wave]
    query = opening[0] if state is None else state[0]
    row_count = query.shape[0]
    heads = query.shape[1] // HD
    shapes = [
        ((heads, row_count, 128), F32),
        ((heads, row_count, 128), F32),
        ((row_count, heads * HD), F32),
    ]
    first = state is None
    kernel = functools.partial(attention_kernel, places, counts, across, req_count, heads, first, parts, len(near))
    if first:
        queries, suffix, gains = opening
        operands = (numbers, in_hbm(queries), in_hbm(suffix), gains, *blocks)
        in_specs = [SMEM, HBM, HBM, VMEM] + [ANY] * len(blocks)
    else:
        operands = (numbers, *state, *blocks, *[in_vmem(part) for part in near])
        in_specs = [SMEM] + [VMEM] * 4 + [ANY] * len(blocks) + [VMEM] * len(near)
    scratch = [
        pltpu.VMEM((len(wave), row_count, 2 * HD), BF16),
        pltpu.SemaphoreType.DMA((len(wave), 2)),
    ]
    states = [jax.ShapeDtypeStruct(shape, dtype) for shape, dtype in shapes]
    if first:
        out_shape = [jax.ShapeDtypeStruct(query.shape, BF16)] + states
        scratch = (
            [pltpu.VMEM(query.shape, BF16)]
            + [pltpu.VMEM((row_count, HD), BF16)] * 2
            + scratch
            + [pltpu.SemaphoreType.DMA((3,))]
        )
    elif parts:
        out_shape = [jax.ShapeDtypeStruct((row_count // parts, query.shape[1]), BF16)] * parts
        scratch = [pltpu.VMEM(shape, dtype) for shape, dtype in shapes] + scratch
    else:
        out_shape = states
    result = pl.pallas_call(
        kernel,
        in_specs=in_specs,
        out_specs=[VMEM] * len(out_shape),
        out_shape=out_shape,
        scratch_shapes=scratch,
        compiler_params=pltpu.CompilerParams(vmem_limit_bytes=mib(7)),
        cost_estimate=pl.CostEstimate(
            flops=8 * row_count * row_count * heads * HD,
            bytes_accessed=mib(4),
            transcendentals=2 * row_count * row_count * heads,
        ),
        name="attend_blocks",
    )(*operands)
    return result if first or parts else [query, *result]


def pick_kernel(lines, numbers, upper_ref, lower_ref, out_ref):
    upper = numbers[0] >= lines

    @pl.when(upper)
    def _():
        out_ref[...] = upper_ref[...]

    @pl.when(jnp.logical_not(upper))
    def _():
        out_ref[...] = lower_ref[...]


def pick(numbers, across, upper, lower):
    return pl.pallas_call(
        functools.partial(pick_kernel, across * LINE // 2),
        in_specs=[SMEM, VMEM, VMEM],
        out_specs=VMEM,
        out_shape=jax.ShapeDtypeStruct(upper.shape, upper.dtype),
        compiler_params=pltpu.CompilerParams(vmem_limit_bytes=mib(4)),
        name="pick",
    )(numbers, upper, lower)


def column_step(width):
    return 512 if width % 512 == 0 else 128


def feed_kernel(pieces, group, planes, *refs):
    refs = list(refs)
    take = lambda count: [refs.pop(0) for _ in range(count)]
    (numbers,), heads_refs, (gains,) = take(1), take(pieces), take(1)
    (gate_ref, up_ref), weight_refs = take(2), take(pieces - 2)
    down_source, residual_ref, *near_sources = take(4)
    (keep_ref, *send_refs), mixed_refs = take(3), take(int(group == 0))
    spare, total_ref, normed_ref, down_ref, sems = refs
    share, width = keep_ref.shape
    hidden = gate_ref.shape[1]
    core_at = lax.rem(numbers[1], CORES)
    first_row = lax.rem(numbers[1] // CORES + group, planes) * CORES * share
    step, unroll = 512, 5

    def columns_of(at, extent):
        return pl.ds(at * extent if isinstance(at, int) else pl.multiple_of(at * extent, extent), extent)

    residual_copies = []
    for tile in range(CORES):
        target = pl.multiple_of(jnp.where(core_at == tile, 0, share), share)
        residual_copies.append(
            pltpu.make_async_copy(
                residual_ref.at[pl.ds(pl.multiple_of(first_row + tile * share, share), share)],
                spare.at[pl.ds(target, share), pl.ds(0, width)],
                sems.at[tile],
            )
        )
    depth = near_sources[0].shape[0]
    near_copies = [
        pltpu.make_async_copy(source, down_ref.at[pl.ds(at * depth, depth)], sems.at[CORES + at])
        for at, source in enumerate(near_sources)
    ]
    down_copies = [
        pltpu.make_async_copy(down_source.at[rows], down_ref.at[rows], sems.at[CORES + 2 + at])
        for at, rows in enumerate((pl.ds(0, 2 * depth), pl.ds(2 * depth, hidden - 2 * depth)))
    ]
    for copy in [*near_copies, *residual_copies, down_copies[1]]:
        copy.start()
    wide = column_step(width)

    @pl.loop(0, width // wide)
    def _(at):
        columns = columns_of(at, wide)
        total = jnp.dot(heads_refs[2][...], weight_refs[0][:, columns], preferred_element_type=F32)
        for piece in range(3, pieces):
            total += jnp.dot(
                heads_refs[piece][...], weight_refs[piece - 2][:, columns], preferred_element_type=F32
            )
        total_ref[:, columns] = total

    for copy in near_copies:
        copy.wait()

    @pl.loop(0, width // wide)
    def _(at):
        columns = columns_of(at, wide)
        total = total_ref[:, columns]
        for piece in range(2):
            total += jnp.dot(
                heads_refs[piece][...],
                down_ref[piece * depth : (piece + 1) * depth, columns],
                preferred_element_type=F32,
            )
        total_ref[:, columns] = total

    down_copies[0].start()
    for copy in residual_copies:
        copy.wait()
    extent = min(64, share)

    @pl.loop(0, CORES * share // extent)
    def _(at):
        rows = pl.ds(pl.multiple_of(at * extent, extent), extent)
        source = lax.rem(at * extent + core_at * share, CORES * share)
        total = total_ref[pl.ds(pl.multiple_of(source, extent), extent), :]
        mixed = spare[rows, :width].astype(F32) + rms(total) * gains[0:1, :]
        normed_ref[rows, :] = (rms(mixed) * gains[1:2, :]).astype(BF16)
        for mixed_ref in mixed_refs:

            @pl.when(at < share // extent)
            def _():
                mixed_ref[rows, :] = mixed

    @pl.loop(0, hidden // step, unroll=unroll)
    def _(at):
        columns = columns_of(at, step)
        gate = jnp.dot(normed_ref[...], gate_ref[:, columns], preferred_element_type=F32)
        upward = jnp.dot(normed_ref[...], up_ref[:, columns], preferred_element_type=F32)
        spare[:, columns] = (jax.nn.gelu(gate, approximate=True) * upward).astype(BF16)

    for copy in down_copies:
        copy.wait()

    @pl.loop(0, width // step, unroll=unroll)
    def _(at):
        columns = columns_of(at, step)
        down = jnp.dot(spare[:, :hidden], down_ref[:, columns], preferred_element_type=F32)
        keep_ref[:, columns] = down[:share]
        for at_send, send_ref in enumerate(send_refs):
            begin = share + at_send * send_ref.shape[0]
            send_ref[:, columns] = down[begin : begin + send_ref.shape[0]].astype(BF16)


def feed_rows(
    numbers, group, planes, residual, heads_parts, near_weights, far_weights, gains, feed_weights
):
    pieces = len(heads_parts)
    rows, depth = heads_parts[0].shape
    width = residual.shape[1]
    share = rows // CORES
    hidden = feed_weights[0].shape[1]
    return pl.pallas_call(
        functools.partial(feed_kernel, pieces, group, planes),
        in_specs=[SMEM] + [VMEM] * (2 * pieces + 1) + [HBM] * 4,
        out_specs=[VMEM] * (3 + (group == 0)),
        out_shape=[pltpu.VMEM((share, width), F32)]
        + [pltpu.VMEM((share // 2, width), BF16)] * 2
        + [pltpu.VMEM((share, width), F32)] * (group == 0),
        scratch_shapes=[
            pltpu.VMEM((rows, max(width, hidden)), BF16),
            pltpu.VMEM((rows, width), F32),
            pltpu.VMEM((rows, width), BF16),
            pltpu.VMEM((hidden, width), BF16),
            pltpu.SemaphoreType.DMA((CORES + 4,)),
        ],
        compiler_params=pltpu.CompilerParams(vmem_limit_bytes=mib(FEED_LIMIT)),
        cost_estimate=pl.CostEstimate(
            flops=2 * rows * width * (pieces * heads_parts[0].shape[1] + 3 * hidden),
            bytes_accessed=mib(16),
            transcendentals=rows * hidden,
        ),
        name="feed_rows",
    )(
        numbers,
        *heads_parts,
        gains,
        *[in_vmem(part) for part in (*feed_weights[:2], *far_weights)],
        *[in_hbm(part) for part in (feed_weights[2], residual, *near_weights)],
    )


def join_kernel(keep_ref, *refs):
    out_ref = refs[-1]
    half = keep_ref.shape[0] // 2
    for at in range(2):
        rows = slice(at * half, (at + 1) * half)
        out_ref[rows, :] = (keep_ref[rows, :] + refs[at][...].astype(F32)).astype(BF16)


def join(keep, other):
    return pl.pallas_call(
        join_kernel,
        out_shape=jax.ShapeDtypeStruct(keep.shape, BF16),
        compiler_params=pltpu.CompilerParams(vmem_limit_bytes=mib(8)),
        name="join",
    )(keep, *other)


def fold_kernel(keep_ref, *refs):
    total = keep_ref[...]
    for other in refs[:-1]:
        total = total + other[...].astype(F32)
    refs[-1][...] = total


def fold(keep, arrived):
    return pl.pallas_call(
        fold_kernel,
        out_shape=jax.ShapeDtypeStruct(keep.shape, F32),
        compiler_params=pltpu.CompilerParams(vmem_limit_bytes=mib(7)),
        name="fold",
    )(keep, *arrived)


def finish_kernel(mixed_ref, total_ref, *refs):
    gains_ref, out_ref = refs[-2:]
    half = total_ref.shape[0] // 2
    for at in range(2):
        rows = slice(at * half, (at + 1) * half)
        total = total_ref[rows, :] + refs[at][...].astype(F32)
        out_ref[rows, :] = (mixed_ref[rows, :] + rms(total) * gains_ref[2:3, :]).astype(BF16)


def finish(mixed, total, other, gains):
    return pl.pallas_call(
        finish_kernel,
        out_shape=jax.ShapeDtypeStruct(mixed.shape, BF16),
        compiler_params=pltpu.CompilerParams(vmem_limit_bytes=mib(7)),
        name="finish",
    )(mixed, total, *other, gains)


def local(
    queries,
    suffix_kv,
    prefix_cache,
    q_gain,
    k_gain,
    lengths,
    group_of,
    owner_order,
    residual,
    w_out,
    attn_gain,
    ffn_in_gain,
    ffn_out_gain,
    w_gate,
    w_up,
    w_down,
):
    req_count = lax.axis_size("req")
    tok_count = lax.axis_size("tok")
    req_index = lax.axis_index("req")
    tok_index = lax.axis_index("tok")
    across = req_count // LINE
    planes = tok_count // CORES
    row_count = queries.shape[0]
    share = row_count // tok_count
    heads_here = queries.shape[1] // HD
    head_ratio = H // KVH
    kv_first = tok_index * heads_here // head_ratio
    kv_width = KVH * HD

    def head_columns(rows_in, which):
        return lax.dynamic_slice_in_dim(rows_in, which * kv_width + kv_first * HD, HD, 1)

    def move(values_in, lines, shift=0):
        pairs = [
            (source * across + col, target * across + (col + shift) % across)
            for source, target in lines
            for col in range(across)
        ]
        return lax.ppermute(values_in, "req", pairs)

    def other_core(values_in):
        return lax.ppermute(values_in, "tok", [(at, at ^ 1) for at in range(tok_count)])

    def plane_shift(values_in, shift):
        return lax.ppermute(
            values_in, "tok", [(at, (at + CORES * shift) % tok_count) for at in range(tok_count)]
        )

    own_block = jnp.concatenate([head_columns(prefix_cache, 0), head_columns(prefix_cache, 1)], axis=1)
    where = jnp.stack([req_index, tok_index, kv_first]).astype(jnp.int32)
    numbers = jnp.concatenate([where, group_of, owner_order, lengths[0]])
    gains = jnp.stack([attn_gain, ffn_in_gain, ffn_out_gain])
    numbers, gains = lax.optimization_barrier((numbers, gains))
    opening = (queries, suffix_kv, jnp.stack([q_gain, k_gain]))
    attention_on = functools.partial(attention_call, numbers, across, req_count)
    shifts = range(1, across)
    every = [(line, line) for line in range(LINE)]

    def across_all(block, table, lines=every):
        return [([move(block, lines, shift)], table, shift) for shift in shifts]

    w_far, own_block = lax.optimization_barrier((w_out, own_block))
    left = move(own_block, [(0, 1), (1, 2), (2, 3)])
    right = move(own_block, [(1, 0), (2, 1), (3, 2)])
    crossed = across_all(own_block, (0, 1, 2, 3))
    plane_weights = [w_out] + [plane_shift(w_far, shift) for shift in range(1, planes)]
    state = attention_on(opening, None, [([own_block], (0, 1, 2, 3), 0)], 0)

    first = [([left], (-1, 0, 1, 2), 0), ([right], (1, 2, 3, -1), 0)] + crossed
    left, right, _ = lax.optimization_barrier((left, right, state[1]))
    onward = move(left, [(1, 2), (2, 3)])
    back = move(right, [(2, 1), (1, 0)])
    second = [([onward], (-1, -1, 0, 1), 0), ([back], (2, 3, -1, -1), 0)]
    second += across_all(pick(numbers, across, left, right), (1, 2, 1, 2))
    second += [
        ([move(block, [(0, 1), (3, 2)])], (-1, 0, 3, -1), shift) for [block], _, shift in crossed
    ]
    state = attention_on(None, state, first, 0)

    onward, back, _ = lax.optimization_barrier((onward, back, state[1]))
    far = pick(numbers, across, onward, back)
    last = move(far, [(2, 3), (1, 0)])
    third = across_all(far, (2, 3, 0, 1))
    state = attention_on(None, state, second, 0)

    last, _ = lax.optimization_barrier((last, state[1]))
    middle = last.shape[0] // 2
    table = (3, -1, -1, 0)
    fourth = []
    for [block], _, shift in third:
        halves = [move(last[:middle], [(0, 0), (3, 3)], shift), move(block[middle:], [(2, 3), (1, 0)])]
        fourth.append((halves, table, shift))
    state = attention_on(None, state, [([last], table, 0)] + third, 0)
    attention = attention_on(None, state, fourth, planes)
    plane_weights[1:], attention = lax.optimization_barrier((plane_weights[1:], attention))

    weight_parts = [[part, other_core(part)] for part in plane_weights]
    far_weights = [part for parts in weight_parts[1:] for part in parts]
    order = list(range(planes - 1, -1, -1))
    far_heads = {}
    previous = None
    for group in order:
        sent = [attention[(group + shift) % planes] for shift in range(1, planes)]
        if previous is not None:
            sent, previous = lax.optimization_barrier((sent, previous))
        previous = [plane_shift(part, shift) for shift, part in enumerate(sent, 1)]
        far_heads[group] = previous
    own_heads = [[attention[group], other_core(attention[group])] for group in range(planes)]

    def rows_of(group):
        heads_parts = list(own_heads[group])
        for part in far_heads[group]:
            heads_parts += [part, other_core(part)]
        return feed_rows(
            numbers,
            group,
            planes,
            residual,
            heads_parts,
            weight_parts[0],
            far_weights,
            gains,
            (w_gate, w_up, w_down),
        )

    keep, *send = rows_of(order[0])
    arrived = []
    for group, later in zip(order, order[1:]):
        joined = join(keep, [other_core(part) for part in send])
        own_heads[later], joined = lax.optimization_barrier((own_heads[later], joined))
        arrived.append(plane_shift(joined, group))
        keep, *send = rows_of(later)
    *send, mixed = send
    send, arrived = lax.optimization_barrier((send, arrived))
    other = [other_core(part) for part in send]
    return finish(mixed, fold(keep, arrived), other, gains)


def solution(mesh):
    in_specs = (
        P("req", "tok"),
        P("req", None),
        P("req", None),
        P(),
        P(),
        P("req", None),
        P(),
        P(),
        P("req", None),
        P("tok", None),
        P(),
        P(),
        P(),
        P(None, "tok"),
        P(None, "tok"),
        P("tok", None),
    )
    out_specs = P(("req", "tok"), None)
    return jax.shard_map(local, mesh=mesh, in_specs=in_specs, out_specs=out_specs, check_vma=False)
```

profile of v0, /device:TPU:0, one launch (start us, length us, event | category | flops | bytes accessed | tf_op | source)
XLA Modules:
  0.0 124.3 jit_solution(16556094530834703928)
XLA Ops:
  0.0 1.1 constant_dynamic-slice_fusion.1
  1.1 0.8 pad_maximum_fusion.refs_4_
  1.9 3.0 %collective-permute-start = (bf16[512,2560]{1,0:T(8,128)(2,1)}, bf16[512,2560]{1,0:T(8,128)(2,1)S(1)}, u32[]{:S(2)}, u32[]{:S(2)}) collective-permute-start(bf16[512,2560]{1,0:T(8,128)(2,1)} %refs_12_.3), channel_id=1, source_target_pairs={{0,2},{1,3},{2,0},{3,1},{4,6},{5,7},{6,4},{7,5},{8,10},{9,11},{10,... | collective-permute-start | bytes 7864328 | tf_op jit(solution)/shard_map/ppermute | solution.py:509
  4.9 1.5 %collective-permute-start.3 = (bf16[512,512]{1,0:T(8,128)(2,1)}, bf16[512,512]{1,0:T(8,128)(2,1)}, u32[]{:S(2)}, u32[]{:S(2)}) collective-permute-start(bf16[512,512]{1,0:T(8,128)(2,1)} %pad_maximum_fusion.refs_4_), channel_id=1, source_target_pairs={{0,4},{4,0},{8,12},{12,8},{16,20},{20,16},{24,28},{28,24},{1,5},{5... | collective-permute-start | bytes 1572872 | tf_op jit(solution)/shard_map/ppermute | solution.py:503
  6.4 1.3 %collective-permute-start.2 = (bf16[512,512]{1,0:T(8,128)(2,1)}, bf16[512,512]{1,0:T(8,128)(2,1)S(1)}, u32[]{:S(2)}, u32[]{:S(2)}) collective-permute-start(bf16[512,512]{1,0:T(8,128)(2,1)} %pad_maximum_fusion.refs_4_), channel_id=1, source_target_pairs={{8,0},{12,4},{16,8},{20,12},{24,16},{28,20},{9,1},{13,5},{17,9},{2... | collective-permute-start | bytes 1572872 | tf_op jit(solution)/shard_map/ppermute | solution.py:503
  7.7 5.4 %collective-permute-start.1 = (bf16[512,512]{1,0:T(8,128)(2,1)}, bf16[512,512]{1,0:T(8,128)(2,1)}, u32[]{:S(2)}, u32[]{:S(2)}) collective-permute-start(bf16[512,512]{1,0:T(8,128)(2,1)} %pad_maximum_fusion.refs_4_), channel_id=1, source_target_pairs={{0,8},{4,12},{8,16},{12,20},{16,24},{20,28},{1,9},{5,13},{9,17},{1... | collective-permute-start | bytes 1572872 | tf_op jit(solution)/shard_map/ppermute | solution.py:503
  13.0 0.7 stack.33
  13.8 0.7 stack.34
  14.5 0.7 stack.35
  15.2 0.8 concatenate.6.refs_0_.numbers
  15.9 0.6 pad_maximum_fusion.1.refs_5_.refs_2_
  16.6 0.7 pad_maximum_fusion.2.refs_3_
  17.3 5.4 %attend_blocks.5 = (bf16[512,512]{1,0:T(8,128)(2,1)S(1)}, f32[2,512,128]{2,1,0:T(8,128)S(1)}, f32[2,512,128]{2,1,0:T(8,128)S(1)}, f32[512,512]{1,0:T(8,128)S(1)}) custom-call(s32[22]{0:T(128)S(1)} %concatenate.6.refs_0_.numbers, bf16[512,512]{1,0:T(8,128)(2,1)} %refs_1_.1, bf16[512,2048]{1,0:T(8,128)(2,1)} %refs_2_.1, ...), custom_call_target="tpu_custom_call" | custom-call | flops 1073741824 | bytes 4194304 | tf_op jit(solution)/shard_map/attend_blocks/pallas_call | solution.py:227
  22.8 0.7 collective-permute-start.4
  23.5 1.3 %collective-permute-start.5 = (bf16[512,512]{1,0:T(8,128)(2,1)S(1)}, bf16[512,512]{1,0:T(8,128)(2,1)S(1)}, u32[]{:S(2)}, u32[]{:S(2)}) collective-permute-start(bf16[512,512]{1,0:T(8,128)(2,1)S(1)} %collective-permute-done.2.refs_6_.lower_ref), channel_id=1, source_target_pairs={{16,8},{20,12},{8,0},{12,4},{17,9},{21,13},{9,1},{13,5},{18,10},{2... | collective-permute-start | bytes 1572872 | tf_op jit(solution)/shard_map/ppermute | solution.py:503
  24.8 1.1 pick.2
  25.9 0.6 collective-permute-start.6
  26.5 7.9 %collective-permute-start.7 = (bf16[512,512]{1,0:T(8,128)(2,1)}, bf16[512,512]{1,0:T(8,128)(2,1)S(1)}, u32[]{:S(2)}, u32[]{:S(2)}) collective-permute-start(bf16[512,512]{1,0:T(8,128)(2,1)} %collective-permute-done.3.refs_7_), channel_id=1, source_target_pairs={{0,8},{4,12},{24,16},{28,20},{1,9},{5,13},{25,17},{29,21},{2,10},{... | collective-permute-start | bytes 1572872 | tf_op jit(solution)/shard_map/ppermute | solution.py:503
  34.4 2.8 %attend_blocks.6 = (f32[2,512,128]{2,1,0:T(8,128)S(1)}, f32[2,512,128]{2,1,0:T(8,128)S(1)}, f32[512,512]{1,0:T(8,128)S(1)}) custom-call(s32[22]{0:T(128)S(1)} %concatenate.6.refs_0_.numbers, bf16[512,512]{1,0:T(8,128)(2,1)S(1)} %get-tuple-element.49.refs_1_, f32[2,512,128]{2,1,0:T(8,128)S(1)} %get-tuple-element.50.refs_2_, ...), custom_call_target="tpu_custom_call" | custom-call | flops 1073741824 | bytes 4194304 | tf_op jit(solution)/shard_map/attend_blocks/pallas_call | solution.py:227
  37.3 3.4 %collective-permute-done.5.refs_6_.lower_ref = bf16[512,512]{1,0:T(8,128)(2,1)S(1)} collective-permute-done((bf16[512,512]{1,0:T(8,128)(2,1)S(1)}, bf16[512,512]{1,0:T(8,128)(2,1)S(1)}, u32[]{:S(2)}, u32[]{:S(2)}) %collective-permute-start.5) | collective-permute-done | bytes 524320 | tf_op jit(solution)/shard_map/ppermute | solution.py:503
  40.6 0.6 pick.3
  41.2 0.6 collective-permute-start.9
  41.8 1.3 %collective-permute-start.8 = (bf16[512,512]{1,0:T(8,128)(2,1)S(1)}, bf16[512,512]{1,0:T(8,128)(2,1)S(1)}, u32[]{:S(2)}, u32[]{:S(2)}) collective-permute-start(bf16[512,512]{1,0:T(8,128)(2,1)S(1)} %pick.3), channel_id=1, source_target_pairs={{16,24},{20,28},{8,0},{12,4},{17,25},{21,29},{9,1},{13,5},{18,26},... | collective-permute-start | bytes 1572872 | tf_op jit(solution)/shard_map/ppermute | solution.py:503
  43.1 0.4 collective-permute-done.7.refs_8_
  43.5 2.9 %attend_blocks.7 = (f32[2,512,128]{2,1,0:T(8,128)S(1)}, f32[2,512,128]{2,1,0:T(8,128)S(1)}, f32[512,512]{1,0:T(8,128)S(1)}) custom-call(s32[22]{0:T(128)S(1)} %concatenate.6.refs_0_.numbers, bf16[512,512]{1,0:T(8,128)(2,1)S(1)} %get-tuple-element.49.refs_1_, f32[2,512,128]{2,1,0:T(8,128)S(1)} %get-tuple-element.53.refs_2_, ...), custom_call_target="tpu_custom_call" | custom-call | flops 1073741824 | bytes 4194304 | tf_op jit(solution)/shard_map/attend_blocks/pallas_call | solution.py:227
  46.4 5.8 %collective-permute-done.9.refs_6_ = bf16[512,512]{1,0:T(8,128)(2,1)S(1)} collective-permute-done((bf16[512,512]{1,0:T(8,128)(2,1)S(1)}, bf16[512,512]{1,0:T(8,128)(2,1)S(1)}, u32[]{:S(2)}, u32[]{:S(2)}) %collective-permute-start.9) | collective-permute-done | bytes 524320 | tf_op jit(solution)/shard_map/ppermute | solution.py:503
  52.3 1.3 %collective-permute-start.11 = (bf16[256,512]{1,0:T(8,128)(2,1)S(1)}, bf16[256,512]{1,0:T(8,128)(2,1)S(1)}, u32[]{:S(2)}, u32[]{:S(2)}) collective-permute-start(bf16[256,512]{1,0:T(8,128)(2,1)S(1)} %slice.8), channel_id=1, source_target_pairs={{16,24},{20,28},{8,0},{12,4},{17,25},{21,29},{9,1},{13,5},{18,26},... | collective-permute-start | bytes 786440 | tf_op jit(solution)/shard_map/ppermute | solution.py:503
  53.6 1.2 collective-permute-done.8.refs_5_
  54.8 4.4 %collective-permute-start.10 = (bf16[256,512]{1,0:T(8,128)(2,1)S(1)}, bf16[256,512]{1,0:T(8,128)(2,1)S(1)}, u32[]{:S(2)}, u32[]{:S(2)}) collective-permute-start(bf16[256,512]{1,0:T(8,128)(2,1)S(1)} %slice.6), channel_id=1, source_target_pairs={{0,4},{4,0},{24,28},{28,24},{1,5},{5,1},{25,29},{29,25},{2,6},{6,2... | collective-permute-start | bytes 786440 | tf_op jit(solution)/shard_map/ppermute | solution.py:503
  59.2 3.0 %attend_blocks.8 = (f32[2,512,128]{2,1,0:T(8,128)S(1)}, f32[2,512,128]{2,1,0:T(8,128)S(1)}, f32[512,512]{1,0:T(8,128)S(1)}) custom-call(s32[22]{0:T(128)S(1)} %concatenate.6.refs_0_.numbers, bf16[512,512]{1,0:T(8,128)(2,1)S(1)} %get-tuple-element.49.refs_1_, f32[2,512,128]{2,1,0:T(8,128)S(1)} %get-tuple-element.58.refs_2_, ...), custom_call_target="tpu_custom_call" | custom-call | flops 1073741824 | bytes 4194304 | tf_op jit(solution)/shard_map/attend_blocks/pallas_call | solution.py:227
  62.2 1.2 %collective-permute-done.10.refs_5_ = bf16[256,512]{1,0:T(8,128)(2,1)S(1)} collective-permute-done((bf16[256,512]{1,0:T(8,128)(2,1)S(1)}, bf16[256,512]{1,0:T(8,128)(2,1)S(1)}, u32[]{:S(2)}, u32[]{:S(2)}) %collective-permute-start.10) | collective-permute-done | bytes 262176 | tf_op jit(solution)/shard_map/ppermute | solution.py:503
  63.5 0.9 attend_blocks.9
  64.5 0.6 collective-permute-start.14
  65.3 8.0 %collective-permute-done.14.refs_3_ = bf16[256,512]{1,0:T(8,128)(2,1)S(1)} collective-permute-done((bf16[256,512]{1,0:T(8,128)(2,1)S(1)}, bf16[256,512]{1,0:T(8,128)(2,1)S(1)}, u32[]{:S(2)}, u32[]{:S(2)}) %collective-permute-start.14) | collective-permute-done | bytes 262176 | tf_op jit(solution)/shard_map/ppermute | solution.py:509
  73.2 0.5 collective-permute-start.20
  73.8 1.0 collective-permute-done.15.refs_4_
  74.8 0.4 copy-done.7
  75.5 4.7 %copy-done.1 = bf16[2560,2560]{1,0:T(8,128)(2,1)S(1)} copy-done((bf16[2560,2560]{1,0:T(8,128)(2,1)S(1)}, bf16[2560,2560]{1,0:T(8,128)(2,1)}, u32[]{:S(2)}) %copy-start.1) | copy-done | bytes 13107224
  80.2 17.8 %feed_rows.2 = (f32[128,2560]{1,0:T(8,128)S(1)}, bf16[64,2560]{1,0:T(8,128)(2,1)S(1)}, bf16[64,2560]{1,0:T(8,128)(2,1)S(1)}) custom-call(s32[22]{0:T(128)} %copy-done.5, bf16[256,512]{1,0:T(8,128)(2,1)} %copy-done.4, bf16[256,512]{1,0:T(8,128)(2,1)} %copy-done.12, bf16[256,512]{1,0:T(8,128)(2,1)} %copy-done.11, bf16[256,512]{1,0:T(8,128)(2,1)} %copy-done.13, ...), custom_call_target="tpu_custom_call" | custom-call | flops 12750684160 | bytes 16777216 | tf_op jit(solution)/shard_map/feed_rows/pallas_call | solution.py:382
  99.1 0.6 collective-permute-done.18.refs_0_
  99.7 0.5 collective-permute-done.19.refs_1_
  100.5 1.4 %collective-permute-start.22 = (bf16[128,2560]{1,0:T(8,128)(2,1)S(1)}, bf16[128,2560]{1,0:T(8,128)(2,1)S(1)}, u32[]{:S(2)}, u32[]{:S(2)}) collective-permute-start(bf16[128,2560]{1,0:T(8,128)(2,1)S(1)} %join.1), channel_id=1, source_target_pairs={{0,2},{1,3},{2,0},{3,1},{4,6},{5,7},{6,4},{7,5},{8,10},{9,11},{10,... | collective-permute-start | bytes 1966088 | tf_op jit(solution)/shard_map/ppermute | solution.py:509
  102.0 0.7 copy-done.10
  102.7 18.1 %feed_rows.3 = (f32[128,2560]{1,0:T(8,128)S(1)}, bf16[64,2560]{1,0:T(8,128)(2,1)S(1)}, bf16[64,2560]{1,0:T(8,128)(2,1)S(1)}, f32[128,2560]{1,0:T(8,128)S(1)}) custom-call(s32[22]{0:T(128)} %copy-done.5, bf16[256,512]{1,0:T(8,128)(2,1)} %copy-done.3, bf16[256,512]{1,0:T(8,128)(2,1)} %copy-done.9, bf16[256,512]{1,0:T(8,128)(2,1)} %copy-done.8, ...), custom_call_target="tpu_custom_call" | custom-call | flops 12750684160 | bytes 16777216 | tf_op jit(solution)/shard_map/feed_rows/pallas_call | solution.py:382
  120.9 0.5 collective-permute-start.24
  121.5 1.0 collective-permute-done.23.refs_0_
  122.5 0.5 collective-permute-done.24.refs_1_
  123.0 1.3 %finish.1 = bf16[128,2560]{1,0:T(8,128)(2,1)} custom-call(f32[128,2560]{1,0:T(8,128)S(1)} %get-tuple-element.79.mixed_ref, f32[128,2560]{1,0:T(8,128)S(1)} %fold.1.total_ref, bf16[64,2560]{1,0:T(8,128)(2,1)S(1)} %collective-permute-done.23.refs_0_, bf16[64,2560]{1,0:T(8,128)(2,1)S(1)} %collective-permute-done.24.refs_1_, f32[3,2560]{1,0:T(4,128)S(1)} %copy-done.2), custom_call_target="tpu_custom_call" | custom-call | tf_op jit(solution)/shard_map/finish/pallas_call | solution.py:455
  (52 shorter events, 2.5 us)
Async XLA Ops:
  1.9 62.5 %collective-permute-start = (bf16[512,2560]{1,0:T(8,128)(2,1)}, bf16[512,2560]{1,0:T(8,128)(2,1)S(1)}, u32[]{:S(2)}, u32[]{:S(2)}) collective-permute-start(bf16[512,2560]{1,0:T(8,128)(2,1)} %refs_12_.3), channel_id=1, source_target_pairs={{0,2},{1,3},{2,0},{3,1},{4,6},{5,7},{6,4},{7,5},{8,10},{9,11},{10,... | collective-permute-start | bytes 7864328 | tf_op jit(solution)/shard_map/ppermute | solution.py:509
  4.9 21.7 %collective-permute-start.3 = (bf16[512,512]{1,0:T(8,128)(2,1)}, bf16[512,512]{1,0:T(8,128)(2,1)}, u32[]{:S(2)}, u32[]{:S(2)}) collective-permute-start(bf16[512,512]{1,0:T(8,128)(2,1)} %pad_maximum_fusion.refs_4_), channel_id=1, source_target_pairs={{0,4},{4,0},{8,12},{12,8},{16,20},{20,16},{24,28},{28,24},{1,5},{5... | collective-permute-start | bytes 1572872 | tf_op jit(solution)/shard_map/ppermute | solution.py:503
  6.4 16.3 %collective-permute-start.2 = (bf16[512,512]{1,0:T(8,128)(2,1)}, bf16[512,512]{1,0:T(8,128)(2,1)S(1)}, u32[]{:S(2)}, u32[]{:S(2)}) collective-permute-start(bf16[512,512]{1,0:T(8,128)(2,1)} %pad_maximum_fusion.refs_4_), channel_id=1, source_target_pairs={{8,0},{12,4},{16,8},{20,12},{24,16},{28,20},{9,1},{13,5},{17,9},{2... | collective-permute-start | bytes 1572872 | tf_op jit(solution)/shard_map/ppermute | solution.py:503
  7.7 15.2 %collective-permute-start.1 = (bf16[512,512]{1,0:T(8,128)(2,1)}, bf16[512,512]{1,0:T(8,128)(2,1)}, u32[]{:S(2)}, u32[]{:S(2)}) collective-permute-start(bf16[512,512]{1,0:T(8,128)(2,1)} %pad_maximum_fusion.refs_4_), channel_id=1, source_target_pairs={{0,8},{4,12},{8,16},{12,20},{16,24},{20,28},{1,9},{5,13},{9,17},{1... | collective-permute-start | bytes 1572872 | tf_op jit(solution)/shard_map/ppermute | solution.py:503
  15.9 47.5 %copy-start.5 = (s32[22]{0:T(128)}, s32[22]{0:T(128)S(1)}, u32[]{:S(2)}) copy-start(s32[22]{0:T(128)S(1)} %concatenate.6.refs_0_.numbers) | copy-start | bytes 268
  22.8 14.4 %collective-permute-start.4 = (bf16[512,512]{1,0:T(8,128)(2,1)}, bf16[512,512]{1,0:T(8,128)(2,1)S(1)}, u32[]{:S(2)}, u32[]{:S(2)}) collective-permute-start(bf16[512,512]{1,0:T(8,128)(2,1)} %collective-permute-done.1.refs_5_.upper_ref), channel_id=1, source_target_pairs={{8,16},{12,20},{16,24},{20,28},{9,17},{13,21},{17,25},{21,29},{10,... | collective-permute-start | bytes 1572872 | tf_op jit(solution)/shard_map/ppermute | solution.py:503
  23.5 17.1 %collective-permute-start.5 = (bf16[512,512]{1,0:T(8,128)(2,1)S(1)}, bf16[512,512]{1,0:T(8,128)(2,1)S(1)}, u32[]{:S(2)}, u32[]{:S(2)}) collective-permute-start(bf16[512,512]{1,0:T(8,128)(2,1)S(1)} %collective-permute-done.2.refs_6_.lower_ref), channel_id=1, source_target_pairs={{16,8},{20,12},{8,0},{12,4},{17,9},{21,13},{9,1},{13,5},{18,10},{2... | collective-permute-start | bytes 1572872 | tf_op jit(solution)/shard_map/ppermute | solution.py:503
  25.9 17.6 %collective-permute-start.6 = (bf16[512,512]{1,0:T(8,128)(2,1)S(1)}, bf16[512,512]{1,0:T(8,128)(2,1)S(1)}, u32[]{:S(2)}, u32[]{:S(2)}) collective-permute-start(bf16[512,512]{1,0:T(8,128)(2,1)S(1)} %pick.2), channel_id=1, source_target_pairs={{0,4},{4,0},{8,12},{12,8},{16,20},{20,16},{24,28},{28,24},{1,5},{5... | collective-permute-start | bytes 1572872 | tf_op jit(solution)/shard_map/ppermute | solution.py:503
  26.5 17.0 %collective-permute-start.7 = (bf16[512,512]{1,0:T(8,128)(2,1)}, bf16[512,512]{1,0:T(8,128)(2,1)S(1)}, u32[]{:S(2)}, u32[]{:S(2)}) collective-permute-start(bf16[512,512]{1,0:T(8,128)(2,1)} %collective-permute-done.3.refs_7_), channel_id=1, source_target_pairs={{0,8},{4,12},{24,16},{28,20},{1,9},{5,13},{25,17},{29,21},{2,10},{... | collective-permute-start | bytes 1572872 | tf_op jit(solution)/shard_map/ppermute | solution.py:503
  34.4 24.7 %copy-start.6 = (bf16[512,2560]{1,0:T(8,128)(2,1)S(1)}, bf16[512,2560]{1,0:T(8,128)(2,1)}, u32[]{:S(2)}) copy-start(bf16[512,2560]{1,0:T(8,128)(2,1)} %refs_12_.3) | copy-start | bytes 7864324
  41.2 11.0 %collective-permute-start.9 = (bf16[512,512]{1,0:T(8,128)(2,1)S(1)}, bf16[512,512]{1,0:T(8,128)(2,1)S(1)}, u32[]{:S(2)}, u32[]{:S(2)}) collective-permute-start(bf16[512,512]{1,0:T(8,128)(2,1)S(1)} %pick.3), channel_id=1, source_target_pairs={{0,4},{4,0},{8,12},{12,8},{16,20},{20,16},{24,28},{28,24},{1,5},{5... | collective-permute-start | bytes 1572872 | tf_op jit(solution)/shard_map/ppermute | solution.py:503
  41.8 12.9 %collective-permute-start.8 = (bf16[512,512]{1,0:T(8,128)(2,1)S(1)}, bf16[512,512]{1,0:T(8,128)(2,1)S(1)}, u32[]{:S(2)}, u32[]{:S(2)}) collective-permute-start(bf16[512,512]{1,0:T(8,128)(2,1)S(1)} %pick.3), channel_id=1, source_target_pairs={{16,24},{20,28},{8,0},{12,4},{17,25},{21,29},{9,1},{13,5},{18,26},... | collective-permute-start | bytes 1572872 | tf_op jit(solution)/shard_map/ppermute | solution.py:503
  43.5 31.9 %copy-start = (bf16[2560,2560]{1,0:T(8,128)(2,1)S(1)}, bf16[2560,2560]{1,0:T(8,128)(2,1)}, u32[]{:S(2)}) copy-start(bf16[2560,2560]{1,0:T(8,128)(2,1)} %refs_6_.3) | copy-start | bytes 39321604
  52.3 9.9 %collective-permute-start.11 = (bf16[256,512]{1,0:T(8,128)(2,1)S(1)}, bf16[256,512]{1,0:T(8,128)(2,1)S(1)}, u32[]{:S(2)}, u32[]{:S(2)}) collective-permute-start(bf16[256,512]{1,0:T(8,128)(2,1)S(1)} %slice.8), channel_id=1, source_target_pairs={{16,24},{20,28},{8,0},{12,4},{17,25},{21,29},{9,1},{13,5},{18,26},... | collective-permute-start | bytes 786440 | tf_op jit(solution)/shard_map/ppermute | solution.py:503
  54.8 8.7 %collective-permute-start.10 = (bf16[256,512]{1,0:T(8,128)(2,1)S(1)}, bf16[256,512]{1,0:T(8,128)(2,1)S(1)}, u32[]{:S(2)}, u32[]{:S(2)}) collective-permute-start(bf16[256,512]{1,0:T(8,128)(2,1)S(1)} %slice.6), channel_id=1, source_target_pairs={{0,4},{4,0},{24,28},{28,24},{1,5},{5,1},{25,29},{29,25},{2,6},{6,2... | collective-permute-start | bytes 786440 | tf_op jit(solution)/shard_map/ppermute | solution.py:503
  59.1 14.6 %collective-permute-start.17 = (bf16[512,2560]{1,0:T(8,128)(2,1)S(1)}, bf16[512,2560]{1,0:T(8,128)(2,1)S(1)}, u32[]{:S(2)}, u32[]{:S(2)}) collective-permute-start(bf16[512,2560]{1,0:T(8,128)(2,1)S(1)} %copy-done.6), channel_id=1, source_target_pairs={{0,1},{1,0},{2,3},{3,2},{4,5},{5,4},{6,7},{7,6},{8,9},{9,8},{10,11... | collective-permute-start | bytes 7864328 | tf_op jit(solution)/shard_map/ppermute | solution.py:506
  64.4 10.4 %copy-start.4 = (bf16[256,512]{1,0:T(8,128)(2,1)}, bf16[256,512]{1,0:T(8,128)(2,1)S(1)}, u32[]{:S(2)}) copy-start(bf16[256,512]{1,0:T(8,128)(2,1)S(1)} %get-tuple-element.78.refs_1_) | copy-start | bytes 786436
  64.4 34.1 %copy-start.3 = (bf16[256,512]{1,0:T(8,128)(2,1)}, bf16[256,512]{1,0:T(8,128)(2,1)S(1)}, u32[]{:S(2)}) copy-start(bf16[256,512]{1,0:T(8,128)(2,1)S(1)} %get-tuple-element.76.refs_1_) | copy-start | bytes 786436
  64.4 10.3 %collective-permute-start.16 = (bf16[512,2560]{1,0:T(8,128)(2,1)S(1)}, bf16[512,2560]{1,0:T(8,128)(2,1)S(1)}, u32[]{:S(2)}, u32[]{:S(2)}) collective-permute-start(bf16[512,2560]{1,0:T(8,128)(2,1)S(1)} %collective-permute-done.refs_8_), channel_id=1, source_target_pairs={{0,1},{1,0},{2,3},{3,2},{4,5},{5,4},{6,7},{7,6},{8,9},{9,8},{10,11... | collective-permute-start | bytes 7864328 | tf_op jit(solution)/shard_map/ppermute | solution.py:506
  64.5 8.7 %collective-permute-start.14 = (bf16[256,512]{1,0:T(8,128)(2,1)S(1)}, bf16[256,512]{1,0:T(8,128)(2,1)S(1)}, u32[]{:S(2)}, u32[]{:S(2)}) collective-permute-start(bf16[256,512]{1,0:T(8,128)(2,1)S(1)} %get-tuple-element.76.refs_1_), channel_id=1, source_target_pairs={{0,2},{1,3},{2,0},{3,1},{4,6},{5,7},{6,4},{7,5},{8,10},{9,11},{10,... | collective-permute-start | bytes 786440 | tf_op jit(solution)/shard_map/ppermute | solution.py:509
  65.1 8.7 %collective-permute-start.13 = (bf16[256,512]{1,0:T(8,128)(2,1)S(1)}, bf16[256,512]{1,0:T(8,128)(2,1)S(1)}, u32[]{:S(2)}, u32[]{:S(2)}) collective-permute-start(bf16[256,512]{1,0:T(8,128)(2,1)S(1)} %get-tuple-element.78.refs_1_), channel_id=1, source_target_pairs={{0,1},{1,0},{2,3},{3,2},{4,5},{5,4},{6,7},{7,6},{8,9},{9,8},{10,11... | collective-permute-start | bytes 786440 | tf_op jit(solution)/shard_map/ppermute | solution.py:506
  73.2 1.6 %copy-start.11 = (bf16[256,512]{1,0:T(8,128)(2,1)}, bf16[256,512]{1,0:T(8,128)(2,1)S(1)}, u32[]{:S(2)}) copy-start(bf16[256,512]{1,0:T(8,128)(2,1)S(1)} %collective-permute-done.14.refs_3_) | copy-start | bytes 786436
  73.2 1.5 %collective-permute-start.15 = (bf16[256,512]{1,0:T(8,128)(2,1)S(1)}, bf16[256,512]{1,0:T(8,128)(2,1)S(1)}, u32[]{:S(2)}, u32[]{:S(2)}) collective-permute-start(bf16[256,512]{1,0:T(8,128)(2,1)S(1)} %collective-permute-done.14.refs_3_), channel_id=1, source_target_pairs={{0,1},{1,0},{2,3},{3,2},{4,5},{5,4},{6,7},{7,6},{8,9},{9,8},{10,11... | collective-permute-start | bytes 786440 | tf_op jit(solution)/shard_map/ppermute | solution.py:506
  73.2 25.5 %collective-permute-start.20 = (bf16[256,512]{1,0:T(8,128)(2,1)S(1)}, bf16[256,512]{1,0:T(8,128)(2,1)S(1)}, u32[]{:S(2)}, u32[]{:S(2)}) collective-permute-start(bf16[256,512]{1,0:T(8,128)(2,1)S(1)} %get-tuple-element.78.refs_1_), channel_id=1, source_target_pairs={{0,2},{1,3},{2,0},{3,1},{4,6},{5,7},{6,4},{7,5},{8,10},{9,11},{10,... | collective-permute-start | bytes 786440 | tf_op jit(solution)/shard_map/ppermute | solution.py:509
  73.8 1.5 %copy-start.7 = (bf16[512,2560]{1,0:T(8,128)(2,1)}, bf16[512,2560]{1,0:T(8,128)(2,1)S(1)}, u32[]{:S(2)}) copy-start(bf16[512,2560]{1,0:T(8,128)(2,1)S(1)} %collective-permute-done.17.refs_13_) | copy-start | bytes 7864324
  73.8 1.6 %copy-start.12 = (bf16[256,512]{1,0:T(8,128)(2,1)}, bf16[256,512]{1,0:T(8,128)(2,1)S(1)}, u32[]{:S(2)}) copy-start(bf16[256,512]{1,0:T(8,128)(2,1)S(1)} %collective-permute-done.13.refs_2_) | copy-start | bytes 786436
  74.8 0.7 copy-start.13
  75.5 4.7 %copy-start.1 = (bf16[2560,2560]{1,0:T(8,128)(2,1)S(1)}, bf16[2560,2560]{1,0:T(8,128)(2,1)}, u32[]{:S(2)}) copy-start(bf16[2560,2560]{1,0:T(8,128)(2,1)} %refs_7_.3) | copy-start | bytes 39321604
  98.0 1.7 %collective-permute-start.18 = (bf16[64,2560]{1,0:T(8,128)(2,1)S(1)}, bf16[64,2560]{1,0:T(8,128)(2,1)S(1)}, u32[]{:S(2)}, u32[]{:S(2)}) collective-permute-start(bf16[64,2560]{1,0:T(8,128)(2,1)S(1)} %get-tuple-element.74), channel_id=1, source_target_pairs={{0,1},{1,0},{2,3},{3,2},{4,5},{5,4},{6,7},{7,6},{8,9},{9,8},{10,11... | collective-permute-start | bytes 983048 | tf_op jit(solution)/shard_map/ppermute | solution.py:506
  98.2 1.9 %collective-permute-start.19 = (bf16[64,2560]{1,0:T(8,128)(2,1)S(1)}, bf16[64,2560]{1,0:T(8,128)(2,1)S(1)}, u32[]{:S(2)}, u32[]{:S(2)}) collective-permute-start(bf16[64,2560]{1,0:T(8,128)(2,1)S(1)} %get-tuple-element.75), channel_id=1, source_target_pairs={{0,1},{1,0},{2,3},{3,2},{4,5},{5,4},{6,7},{7,6},{8,9},{9,8},{10,11... | collective-permute-start | bytes 983048 | tf_op jit(solution)/shard_map/ppermute | solution.py:506
  98.5 2.0 %collective-permute-start.12 = (bf16[256,512]{1,0:T(8,128)(2,1)S(1)}, bf16[256,512]{1,0:T(8,128)(2,1)S(1)}, u32[]{:S(2)}, u32[]{:S(2)}) collective-permute-start(bf16[256,512]{1,0:T(8,128)(2,1)S(1)} %get-tuple-element.76.refs_1_), channel_id=1, source_target_pairs={{0,1},{1,0},{2,3},{3,2},{4,5},{5,4},{6,7},{7,6},{8,9},{9,8},{10,11... | collective-permute-start | bytes 786440 | tf_op jit(solution)/shard_map/ppermute | solution.py:506
  98.7 3.3 %copy-start.8 = (bf16[256,512]{1,0:T(8,128)(2,1)}, bf16[256,512]{1,0:T(8,128)(2,1)S(1)}, u32[]{:S(2)}) copy-start(bf16[256,512]{1,0:T(8,128)(2,1)S(1)} %collective-permute-done.20.refs_3_) | copy-start | bytes 786436
  98.7 3.2 %collective-permute-start.21 = (bf16[256,512]{1,0:T(8,128)(2,1)S(1)}, bf16[256,512]{1,0:T(8,128)(2,1)S(1)}, u32[]{:S(2)}, u32[]{:S(2)}) collective-permute-start(bf16[256,512]{1,0:T(8,128)(2,1)S(1)} %collective-permute-done.20.refs_3_), channel_id=1, source_target_pairs={{0,1},{1,0},{2,3},{3,2},{4,5},{5,4},{6,7},{7,6},{8,9},{9,8},{10,11... | collective-permute-start | bytes 786440 | tf_op jit(solution)/shard_map/ppermute | solution.py:506
  100.5 1.5 %copy-start.9 = (bf16[256,512]{1,0:T(8,128)(2,1)}, bf16[256,512]{1,0:T(8,128)(2,1)S(1)}, u32[]{:S(2)}) copy-start(bf16[256,512]{1,0:T(8,128)(2,1)S(1)} %collective-permute-done.12.refs_2_) | copy-start | bytes 786436
  100.5 20.3 %collective-permute-start.22 = (bf16[128,2560]{1,0:T(8,128)(2,1)S(1)}, bf16[128,2560]{1,0:T(8,128)(2,1)S(1)}, u32[]{:S(2)}, u32[]{:S(2)}) collective-permute-start(bf16[128,2560]{1,0:T(8,128)(2,1)S(1)} %join.1), channel_id=1, source_target_pairs={{0,2},{1,3},{2,0},{3,1},{4,6},{5,7},{6,4},{7,5},{8,10},{9,11},{10,... | collective-permute-start | bytes 1966088 | tf_op jit(solution)/shard_map/ppermute | solution.py:509
  102.0 0.7 copy-start.10
  120.8 2.2 %copy-start.2 = (f32[3,2560]{1,0:T(4,128)S(1)}, f32[3,2560]{1,0:T(4,128)}, u32[]{:S(2)}) copy-start(f32[3,2560]{1,0:T(4,128)} %pad_maximum_fusion.1.refs_5_.refs_2_) | copy-start | bytes 92164
  120.8 1.7 %collective-permute-start.23 = (bf16[64,2560]{1,0:T(8,128)(2,1)S(1)}, bf16[64,2560]{1,0:T(8,128)(2,1)S(1)}, u32[]{:S(2)}, u32[]{:S(2)}) collective-permute-start(bf16[64,2560]{1,0:T(8,128)(2,1)S(1)} %get-tuple-element.85), channel_id=1, source_target_pairs={{0,1},{1,0},{2,3},{3,2},{4,5},{5,4},{6,7},{7,6},{8,9},{9,8},{10,11... | collective-permute-start | bytes 983048 | tf_op jit(solution)/shard_map/ppermute | solution.py:506
  120.9 2.1 %collective-permute-start.24 = (bf16[64,2560]{1,0:T(8,128)(2,1)S(1)}, bf16[64,2560]{1,0:T(8,128)(2,1)S(1)}, u32[]{:S(2)}, u32[]{:S(2)}) collective-permute-start(bf16[64,2560]{1,0:T(8,128)(2,1)S(1)} %get-tuple-element.86), channel_id=1, source_target_pairs={{0,1},{1,0},{2,3},{3,2},{4,5},{5,4},{6,7},{7,6},{8,9},{9,8},{10,11... | collective-permute-start | bytes 983048 | tf_op jit(solution)/shard_map/ppermute | solution.py:506
where the time goes:
time: 126 us; the launch traced here: 124 us
  Pallas kernels  54 us (43%)
  starting transfers between devices  33.6 us (27%)
  waiting for transfers between devices  24 us (19%)
  local copies, waits for them, and re-layouts  10.2 us (8%)
  other arithmetic  2.18 us (2%)
    pallas_call x2, Pallas kernels, feed_rows(): pl.pallas_call(functools.partial(feed_kernel, pieces, group, planes), in_...  35.9 us
    ppermute x11, starting transfers between devices, move(): return lax.ppermute(values_in, 'req', pairs)  26.1 us
    pallas_call x5, Pallas kernels, attention_call(): pl.pallas_call(kernel, in_specs=in_specs, out_specs=[VMEM] * len(out_shap...  15 us
    ppermute x11, waiting for transfers between devices, move(): return lax.ppermute(values_in, 'req', pairs)  12.2 us
    ppermute x4, waiting for transfers between devices, plane_shift(): lax.ppermute(values_in, 'tok', [(at, (at + CORES * shift) % tok_count) fo...  7.99 us
    unnamed x28, local copies, waits for them, and re-layouts  6.17 us
    ppermute x4, starting transfers between devices, plane_shift(): lax.ppermute(values_in, 'tok', [(at, (at + CORES * shift) % tok_count) fo...  5.49 us
    ppermute x10, waiting for transfers between devices, other_core(): lax.ppermute(values_in, 'tok', [(at, at ^ 1) for at in range(tok_count)])  3.82 us
  transfers between devices with their start and end apart: 25, of which 13 were waited for; matrix products, arithmetic and copies ran while one was open for 3% of the time, Pallas kernels for 42%

commit v1 on v0

--- a/solution.py
+++ b/solution.py
@@ -16,7 +16,7 @@
 CORES = 2
 LINE = 4
 NUMBERS = 3
-FEED_LIMIT = 25
+FEED_LIMIT = 38
 BF16 = jnp.bfloat16
 F32 = jnp.float32
 ANY = pl.BlockSpec(memory_space=pl.ANY)
@@ -272,15 +272,16 @@
     refs = list(refs)
     take = lambda count: [refs.pop(0) for _ in range(count)]
     (numbers,), heads_refs, (gains,) = take(1), take(pieces), take(1)
-    (gate_ref, up_ref), weight_refs = take(2), take(pieces - 2)
-    down_source, residual_ref, *near_sources = take(4)
+    (gate_ref,), weight_refs = take(1), take(pieces - 2)
+    up_source, down_source, residual_ref, *near_sources = take(5)
     (keep_ref, *send_refs), mixed_refs = take(3), take(int(group == 0))
-    spare, total_ref, normed_ref, down_ref, sems = refs
+    spare, total_ref, normed_ref, up_ref, down_ref, sems = refs
     share, width = keep_ref.shape
     hidden = gate_ref.shape[1]
     core_at = lax.rem(numbers[1], CORES)
     first_row = lax.rem(numbers[1] // CORES + group, planes) * CORES * share
-    step, unroll = 512, 5
+    unroll = 5
+    step = 512 if hidden % 512 == 0 else 256
 
     def columns_of(at, extent):
         return pl.ds(at * extent if isinstance(at, int) else pl.multiple_of(at * extent, extent), extent)
@@ -304,7 +305,13 @@
         pltpu.make_async_copy(down_source.at[rows], down_ref.at[rows], sems.at[CORES + 2 + at])
         for at, rows in enumerate((pl.ds(0, 2 * depth), pl.ds(2 * depth, hidden - 2 * depth)))
     ]
-    for copy in [*near_copies, *residual_copies, down_copies[1]]:
+    up_copies = [
+        pltpu.make_async_copy(
+            up_source.at[:, pl.ds(begin, step)], up_ref.at[:, pl.ds(begin, step)], sems.at[CORES + 4 + at]
+        )
+        for at, begin in enumerate(range(0, hidden, step))
+    ]
+    for copy in [*near_copies, *residual_copies, *up_copies, down_copies[1]]:
         copy.start()
     wide = column_step(width)
 
@@ -351,10 +358,10 @@
             def _():
                 mixed_ref[rows, :] = mixed
 
-    @pl.loop(0, hidden // step, unroll=unroll)
-    def _(at):
-        columns = columns_of(at, step)
+    for at, copy in enumerate(up_copies):
+        columns = slice(at * step, (at + 1) * step)
         gate = jnp.dot(normed_ref[...], gate_ref[:, columns], preferred_element_type=F32)
+        copy.wait()
         upward = jnp.dot(normed_ref[...], up_ref[:, columns], preferred_element_type=F32)
         spare[:, columns] = (jax.nn.gelu(gate, approximate=True) * upward).astype(BF16)
 
@@ -381,7 +388,7 @@
     hidden = feed_weights[0].shape[1]
     return pl.pallas_call(
         functools.partial(feed_kernel, pieces, group, planes),
-        in_specs=[SMEM] + [VMEM] * (2 * pieces + 1) + [HBM] * 4,
+        in_specs=[SMEM] + [VMEM] * (2 * pieces) + [HBM] * 5,
         out_specs=[VMEM] * (3 + (group == 0)),
         out_shape=[pltpu.VMEM((share, width), F32)]
         + [pltpu.VMEM((share // 2, width), BF16)] * 2
@@ -390,8 +397,9 @@
             pltpu.VMEM((rows, max(width, hidden)), BF16),
             pltpu.VMEM((rows, width), F32),
             pltpu.VMEM((rows, width), BF16),
+            pltpu.VMEM((width, hidden), BF16),
             pltpu.VMEM((hidden, width), BF16),
-            pltpu.SemaphoreType.DMA((CORES + 4,)),
+            pltpu.SemaphoreType.DMA((CORES + 4 + hidden // 256,)),
         ],
         compiler_params=pltpu.CompilerParams(vmem_limit_bytes=mib(FEED_LIMIT)),
         cost_estimate=pl.CostEstimate(
@@ -404,8 +412,8 @@
         numbers,
         *heads_parts,
         gains,
-        *[in_vmem(part) for part in (*feed_weights[:2], *far_weights)],
-        *[in_hbm(part) for part in (feed_weights[2], residual, *near_weights)],
+        *[in_vmem(part) for part in (feed_weights[0], *far_weights)],
+        *[in_hbm(part) for part in (*feed_weights[1:], residual, *near_weights)],
     )
 
 

time: 126 us -> 125 us (level)
  local copies, waits for them, and re-layouts: 10.2 us -> 5.89 us
  waiting for transfers between devices: 24 us -> 26.2 us
  Pallas kernels: 54 us -> 55.8 us
    unnamed x28 -> x26, local copies, waits for them, and re-layouts: 6.17 us -> 1.88 us
    ppermute x11, waiting for transfers between devices: 12.2 us -> 14.4 us  [move(): return lax.ppermute(values_in, 'req', pairs)]
    pallas_call x2, Pallas kernels: 35.9 us -> 37.7 us  [feed_rows(): pl.pallas_call(functools.partial(feed_kernel, pieces, group, planes), in_...]
  transfers between devices with their start and end apart: 25 -> 25, of which waited for: 13 -> 14; matrix products, arithmetic and copies ran while one was open for 3% -> 3% of each run, Pallas kernels for 42% -> 44%
where the time goes in v1:
time: 125 us; the launch traced here: 124 us
  Pallas kernels  55.8 us (45%)
  starting transfers between devices  33.6 us (27%)
  waiting for transfers between devices  26.2 us (21%)
  local copies, waits for them, and re-layouts  5.89 us (5%)
  other arithmetic  2.17 us (2%)
    pallas_call x2, Pallas kernels, feed_rows(): pl.pallas_call(functools.partial(feed_kernel, pieces, group, planes), in_...  37.7 us
    ppermute x11, starting transfers between devices, move(): return lax.ppermute(values_in, 'req', pairs)  26.1 us
    pallas_call x5, Pallas kernels, attention_call(): pl.pallas_call(kernel, in_specs=in_specs, out_specs=[VMEM] * len(out_shap...  14.8 us
    ppermute x11, waiting for transfers between devices, move(): return lax.ppermute(values_in, 'req', pairs)  14.4 us
    ppermute x4, waiting for transfers between devices, plane_shift(): lax.ppermute(values_in, 'tok', [(at, (at + CORES * shift) % tok_count) fo...  7.99 us
    ppermute x4, starting transfers between devices, plane_shift(): lax.ppermute(values_in, 'tok', [(at, (at + CORES * shift) % tok_count) fo...  5.56 us
    ppermute x10, waiting for transfers between devices, other_core(): lax.ppermute(values_in, 'tok', [(at, at ^ 1) for at in range(tok_count)])  3.82 us
  transfers between devices with their start and end apart: 25, of which 14 were waited for; matrix products, arithmetic and copies ran while one was open for 3% of the time, Pallas kernels for 44%

profile of v1, /device:TPU:0, one launch (start us, length us, event | category | flops | bytes accessed | tf_op | source)
XLA Modules:
  0.0 124.0 jit_solution(15565029921685465071)
XLA Ops:
  0.0 1.1 constant_dynamic-slice_fusion.1
  1.1 0.8 pad_maximum_fusion.refs_4_
  1.9 3.0 %collective-permute-start = (bf16[512,2560]{1,0:T(8,128)(2,1)}, bf16[512,2560]{1,0:T(8,128)(2,1)S(1)}, u32[]{:S(2)}, u32[]{:S(2)}) collective-permute-start(bf16[512,2560]{1,0:T(8,128)(2,1)} %refs_12_.3), channel_id=1, source_target_pairs={{0,2},{1,3},{2,0},{3,1},{4,6},{5,7},{6,4},{7,5},{8,10},{9,11},{10,... | collective-permute-start | bytes 7864328 | tf_op jit(solution)/shard_map/ppermute | solution.py:517
  4.9 1.5 %collective-permute-start.3 = (bf16[512,512]{1,0:T(8,128)(2,1)}, bf16[512,512]{1,0:T(8,128)(2,1)}, u32[]{:S(2)}, u32[]{:S(2)}) collective-permute-start(bf16[512,512]{1,0:T(8,128)(2,1)} %pad_maximum_fusion.refs_4_), channel_id=1, source_target_pairs={{0,4},{4,0},{8,12},{12,8},{16,20},{20,16},{24,28},{28,24},{1,5},{5... | collective-permute-start | bytes 1572872 | tf_op jit(solution)/shard_map/ppermute | solution.py:511
  6.4 1.3 %collective-permute-start.2 = (bf16[512,512]{1,0:T(8,128)(2,1)}, bf16[512,512]{1,0:T(8,128)(2,1)S(1)}, u32[]{:S(2)}, u32[]{:S(2)}) collective-permute-start(bf16[512,512]{1,0:T(8,128)(2,1)} %pad_maximum_fusion.refs_4_), channel_id=1, source_target_pairs={{8,0},{12,4},{16,8},{20,12},{24,16},{28,20},{9,1},{13,5},{17,9},{2... | collective-permute-start | bytes 1572872 | tf_op jit(solution)/shard_map/ppermute | solution.py:511
  7.7 5.4 %collective-permute-start.1 = (bf16[512,512]{1,0:T(8,128)(2,1)}, bf16[512,512]{1,0:T(8,128)(2,1)}, u32[]{:S(2)}, u32[]{:S(2)}) collective-permute-start(bf16[512,512]{1,0:T(8,128)(2,1)} %pad_maximum_fusion.refs_4_), channel_id=1, source_target_pairs={{0,8},{4,12},{8,16},{12,20},{16,24},{20,28},{1,9},{5,13},{9,17},{1... | collective-permute-start | bytes 1572872 | tf_op jit(solution)/shard_map/ppermute | solution.py:511
  13.0 0.7 stack.33
  13.8 0.7 stack.34
  14.5 0.7 stack.35
  15.2 0.8 concatenate.6.refs_0_.numbers
  15.9 0.6 pad_maximum_fusion.1.refs_5_.refs_2_
  16.6 0.7 pad_maximum_fusion.2.refs_3_
  17.3 5.3 %attend_blocks.5 = (bf16[512,512]{1,0:T(8,128)(2,1)S(1)}, f32[2,512,128]{2,1,0:T(8,128)S(1)}, f32[2,512,128]{2,1,0:T(8,128)S(1)}, f32[512,512]{1,0:T(8,128)S(1)}) custom-call(s32[22]{0:T(128)S(1)} %concatenate.6.refs_0_.numbers, bf16[512,512]{1,0:T(8,128)(2,1)} %refs_1_.1, bf16[512,2048]{1,0:T(8,128)(2,1)} %refs_2_.1, ...), custom_call_target="tpu_custom_call" | custom-call | flops 1073741824 | bytes 4194304 | tf_op jit(solution)/shard_map/attend_blocks/pallas_call | solution.py:227
  22.8 0.7 collective-permute-start.4
  23.5 1.3 %collective-permute-start.5 = (bf16[512,512]{1,0:T(8,128)(2,1)S(1)}, bf16[512,512]{1,0:T(8,128)(2,1)S(1)}, u32[]{:S(2)}, u32[]{:S(2)}) collective-permute-start(bf16[512,512]{1,0:T(8,128)(2,1)S(1)} %collective-permute-done.2.refs_6_.lower_ref), channel_id=1, source_target_pairs={{16,8},{20,12},{8,0},{12,4},{17,9},{21,13},{9,1},{13,5},{18,10},{2... | collective-permute-start | bytes 1572872 | tf_op jit(solution)/shard_map/ppermute | solution.py:511
  24.8 1.1 pick.2
  25.9 0.6 collective-permute-start.6
  26.5 7.9 %collective-permute-start.7 = (bf16[512,512]{1,0:T(8,128)(2,1)}, bf16[512,512]{1,0:T(8,128)(2,1)S(1)}, u32[]{:S(2)}, u32[]{:S(2)}) collective-permute-start(bf16[512,512]{1,0:T(8,128)(2,1)} %collective-permute-done.3.refs_7_), channel_id=1, source_target_pairs={{0,8},{4,12},{24,16},{28,20},{1,9},{5,13},{25,17},{29,21},{2,10},{... | collective-permute-start | bytes 1572872 | tf_op jit(solution)/shard_map/ppermute | solution.py:511
  34.4 0.8 attend_blocks.6
  35.2 5.4 %collective-permute-done.5.refs_6_.lower_ref = bf16[512,512]{1,0:T(8,128)(2,1)S(1)} collective-permute-done((bf16[512,512]{1,0:T(8,128)(2,1)S(1)}, bf16[512,512]{1,0:T(8,128)(2,1)S(1)}, u32[]{:S(2)}, u32[]{:S(2)}) %collective-permute-start.5) | collective-permute-done | bytes 524320 | tf_op jit(solution)/shard_map/ppermute | solution.py:511
  40.6 0.6 pick.3
  41.2 0.6 collective-permute-start.9
  41.8 1.3 %collective-permute-start.8 = (bf16[512,512]{1,0:T(8,128)(2,1)S(1)}, bf16[512,512]{1,0:T(8,128)(2,1)S(1)}, u32[]{:S(2)}, u32[]{:S(2)}) collective-permute-start(bf16[512,512]{1,0:T(8,128)(2,1)S(1)} %pick.3), channel_id=1, source_target_pairs={{16,24},{20,28},{8,0},{12,4},{17,25},{21,29},{9,1},{13,5},{18,26},... | collective-permute-start | bytes 1572872 | tf_op jit(solution)/shard_map/ppermute | solution.py:511
  43.1 0.4 collective-permute-done.7.refs_8_
  43.5 4.8 %attend_blocks.7 = (f32[2,512,128]{2,1,0:T(8,128)S(1)}, f32[2,512,128]{2,1,0:T(8,128)S(1)}, f32[512,512]{1,0:T(8,128)S(1)}) custom-call(s32[22]{0:T(128)S(1)} %concatenate.6.refs_0_.numbers, bf16[512,512]{1,0:T(8,128)(2,1)S(1)} %get-tuple-element.49.refs_1_, f32[2,512,128]{2,1,0:T(8,128)S(1)} %get-tuple-element.53.refs_2_, ...), custom_call_target="tpu_custom_call" | custom-call | flops 1073741824 | bytes 4194304 | tf_op jit(solution)/shard_map/attend_blocks/pallas_call | solution.py:227
  48.4 3.9 %collective-permute-done.9.refs_6_ = bf16[512,512]{1,0:T(8,128)(2,1)S(1)} collective-permute-done((bf16[512,512]{1,0:T(8,128)(2,1)S(1)}, bf16[512,512]{1,0:T(8,128)(2,1)S(1)}, u32[]{:S(2)}, u32[]{:S(2)}) %collective-permute-start.9) | collective-permute-done | bytes 524320 | tf_op jit(solution)/shard_map/ppermute | solution.py:511
  52.3 1.3 %collective-permute-start.11 = (bf16[256,512]{1,0:T(8,128)(2,1)S(1)}, bf16[256,512]{1,0:T(8,128)(2,1)S(1)}, u32[]{:S(2)}, u32[]{:S(2)}) collective-permute-start(bf16[256,512]{1,0:T(8,128)(2,1)S(1)} %slice.8), channel_id=1, source_target_pairs={{16,24},{20,28},{8,0},{12,4},{17,25},{21,29},{9,1},{13,5},{18,26},... | collective-permute-start | bytes 786440 | tf_op jit(solution)/shard_map/ppermute | solution.py:511
  53.6 1.2 collective-permute-done.8.refs_5_
  54.8 4.4 %collective-permute-start.10 = (bf16[256,512]{1,0:T(8,128)(2,1)S(1)}, bf16[256,512]{1,0:T(8,128)(2,1)S(1)}, u32[]{:S(2)}, u32[]{:S(2)}) collective-permute-start(bf16[256,512]{1,0:T(8,128)(2,1)S(1)} %slice.6), channel_id=1, source_target_pairs={{0,4},{4,0},{24,28},{28,24},{1,5},{5,1},{25,29},{29,25},{2,6},{6,2... | collective-permute-start | bytes 786440 | tf_op jit(solution)/shard_map/ppermute | solution.py:511
  59.2 0.9 attend_blocks.8
  60.5 2.9 %collective-permute-done.10.refs_5_ = bf16[256,512]{1,0:T(8,128)(2,1)S(1)} collective-permute-done((bf16[256,512]{1,0:T(8,128)(2,1)S(1)}, bf16[256,512]{1,0:T(8,128)(2,1)S(1)}, u32[]{:S(2)}, u32[]{:S(2)}) %collective-permute-start.10) | collective-permute-done | bytes 262176 | tf_op jit(solution)/shard_map/ppermute | solution.py:511
  63.5 3.0 %attend_blocks.9 = (bf16[256,512]{1,0:T(8,128)(2,1)S(1)}, bf16[256,512]{1,0:T(8,128)(2,1)S(1)}) custom-call(s32[22]{0:T(128)S(1)} %concatenate.6.refs_0_.numbers, bf16[512,512]{1,0:T(8,128)(2,1)S(1)} %get-tuple-element.49.refs_1_, f32[2,512,128]{2,1,0:T(8,128)S(1)} %get-tuple-element.64.refs_2_, f32[2,512,128]{2,1,0:T(8,128)S(1)} %get-tuple-element.65.refs_3_, ...), custom_call_target="tpu_custom_call" | custom-call | flops 1073741824 | bytes 4194304 | tf_op jit(solution)/shard_map/attend_blocks/pallas_call | solution.py:227
  66.5 0.6 collective-permute-start.14
  67.3 8.0 %collective-permute-done.14.refs_3_ = bf16[256,512]{1,0:T(8,128)(2,1)S(1)} collective-permute-done((bf16[256,512]{1,0:T(8,128)(2,1)S(1)}, bf16[256,512]{1,0:T(8,128)(2,1)S(1)}, u32[]{:S(2)}, u32[]{:S(2)}) %collective-permute-start.14) | collective-permute-done | bytes 262176 | tf_op jit(solution)/shard_map/ppermute | solution.py:517
  75.3 0.5 collective-permute-start.20
  75.8 1.0 collective-permute-done.15.refs_4_
  76.8 0.5 copy-done.6
  77.3 0.6 copy-done.12
  77.9 18.7 %feed_rows.2 = (f32[128,2560]{1,0:T(8,128)S(1)}, bf16[64,2560]{1,0:T(8,128)(2,1)S(1)}, bf16[64,2560]{1,0:T(8,128)(2,1)S(1)}) custom-call(s32[22]{0:T(128)} %copy-done.4, bf16[256,512]{1,0:T(8,128)(2,1)} %copy-done.3, bf16[256,512]{1,0:T(8,128)(2,1)} %copy-done.11, bf16[256,512]{1,0:T(8,128)(2,1)} %copy-done.10, bf16[256,512]{1,0:T(8,128)(2,1)} %copy-done.12, ...), custom_call_target="tpu_custom_call" | custom-call | flops 12750684160 | bytes 16777216 | tf_op jit(solution)/shard_map/feed_rows/pallas_call | solution.py:389
  97.7 0.6 collective-permute-done.18.refs_0_
  98.3 0.5 collective-permute-done.19.refs_1_
  99.2 1.5 %collective-permute-start.22 = (bf16[128,2560]{1,0:T(8,128)(2,1)S(1)}, bf16[128,2560]{1,0:T(8,128)(2,1)S(1)}, u32[]{:S(2)}, u32[]{:S(2)}) collective-permute-start(bf16[128,2560]{1,0:T(8,128)(2,1)S(1)} %join.1), channel_id=1, source_target_pairs={{0,2},{1,3},{2,0},{3,1},{4,6},{5,7},{6,4},{7,5},{8,10},{9,11},{10,... | collective-permute-start | bytes 1966088 | tf_op jit(solution)/shard_map/ppermute | solution.py:517
  100.7 0.7 copy-done.9
  101.4 19.0 %feed_rows.3 = (f32[128,2560]{1,0:T(8,128)S(1)}, bf16[64,2560]{1,0:T(8,128)(2,1)S(1)}, bf16[64,2560]{1,0:T(8,128)(2,1)S(1)}, f32[128,2560]{1,0:T(8,128)S(1)}) custom-call(s32[22]{0:T(128)} %copy-done.4, bf16[256,512]{1,0:T(8,128)(2,1)} %copy-done.2, bf16[256,512]{1,0:T(8,128)(2,1)} %copy-done.8, bf16[256,512]{1,0:T(8,128)(2,1)} %copy-done.7, ...), custom_call_target="tpu_custom_call" | custom-call | flops 12750684160 | bytes 16777216 | tf_op jit(solution)/shard_map/feed_rows/pallas_call | solution.py:389
  120.6 0.5 collective-permute-start.24
  121.2 1.0 collective-permute-done.23.refs_0_
  122.2 0.5 collective-permute-done.24.refs_1_
  122.7 1.3 %finish.1 = bf16[128,2560]{1,0:T(8,128)(2,1)} custom-call(f32[128,2560]{1,0:T(8,128)S(1)} %get-tuple-element.79.mixed_ref, f32[128,2560]{1,0:T(8,128)S(1)} %fold.1.total_ref, bf16[64,2560]{1,0:T(8,128)(2,1)S(1)} %collective-permute-done.23.refs_0_, bf16[64,2560]{1,0:T(8,128)(2,1)S(1)} %collective-permute-done.24.refs_1_, f32[3,2560]{1,0:T(4,128)S(1)} %copy-done.1), custom_call_target="tpu_custom_call" | custom-call | tf_op jit(solution)/shard_map/finish/pallas_call | solution.py:463
  (50 shorter events, 2.7 us)
Async XLA Ops:
  1.9 64.5 %collective-permute-start = (bf16[512,2560]{1,0:T(8,128)(2,1)}, bf16[512,2560]{1,0:T(8,128)(2,1)S(1)}, u32[]{:S(2)}, u32[]{:S(2)}) collective-permute-start(bf16[512,2560]{1,0:T(8,128)(2,1)} %refs_12_.3), channel_id=1, source_target_pairs={{0,2},{1,3},{2,0},{3,1},{4,6},{5,7},{6,4},{7,5},{8,10},{9,11},{10,... | collective-permute-start | bytes 7864328 | tf_op jit(solution)/shard_map/ppermute | solution.py:517
  4.9 21.7 %collective-permute-start.3 = (bf16[512,512]{1,0:T(8,128)(2,1)}, bf16[512,512]{1,0:T(8,128)(2,1)}, u32[]{:S(2)}, u32[]{:S(2)}) collective-permute-start(bf16[512,512]{1,0:T(8,128)(2,1)} %pad_maximum_fusion.refs_4_), channel_id=1, source_target_pairs={{0,4},{4,0},{8,12},{12,8},{16,20},{20,16},{24,28},{28,24},{1,5},{5... | collective-permute-start | bytes 1572872 | tf_op jit(solution)/shard_map/ppermute | solution.py:511
  6.4 16.3 %collective-permute-start.2 = (bf16[512,512]{1,0:T(8,128)(2,1)}, bf16[512,512]{1,0:T(8,128)(2,1)S(1)}, u32[]{:S(2)}, u32[]{:S(2)}) collective-permute-start(bf16[512,512]{1,0:T(8,128)(2,1)} %pad_maximum_fusion.refs_4_), channel_id=1, source_target_pairs={{8,0},{12,4},{16,8},{20,12},{24,16},{28,20},{9,1},{13,5},{17,9},{2... | collective-permute-start | bytes 1572872 | tf_op jit(solution)/shard_map/ppermute | solution.py:511
  7.7 15.2 %collective-permute-start.1 = (bf16[512,512]{1,0:T(8,128)(2,1)}, bf16[512,512]{1,0:T(8,128)(2,1)}, u32[]{:S(2)}, u32[]{:S(2)}) collective-permute-start(bf16[512,512]{1,0:T(8,128)(2,1)} %pad_maximum_fusion.refs_4_), channel_id=1, source_target_pairs={{0,8},{4,12},{8,16},{12,20},{16,24},{20,28},{1,9},{5,13},{9,17},{1... | collective-permute-start | bytes 1572872 | tf_op jit(solution)/shard_map/ppermute | solution.py:511
  15.9 47.5 %copy-start.4 = (s32[22]{0:T(128)}, s32[22]{0:T(128)S(1)}, u32[]{:S(2)}) copy-start(s32[22]{0:T(128)S(1)} %concatenate.6.refs_0_.numbers) | copy-start | bytes 268
  22.8 12.4 %collective-permute-start.4 = (bf16[512,512]{1,0:T(8,128)(2,1)}, bf16[512,512]{1,0:T(8,128)(2,1)S(1)}, u32[]{:S(2)}, u32[]{:S(2)}) collective-permute-start(bf16[512,512]{1,0:T(8,128)(2,1)} %collective-permute-done.1.refs_5_.upper_ref), channel_id=1, source_target_pairs={{8,16},{12,20},{16,24},{20,28},{9,17},{13,21},{17,25},{21,29},{10,... | collective-permute-start | bytes 1572872 | tf_op jit(solution)/shard_map/ppermute | solution.py:511
  23.5 17.1 %collective-permute-start.5 = (bf16[512,512]{1,0:T(8,128)(2,1)S(1)}, bf16[512,512]{1,0:T(8,128)(2,1)S(1)}, u32[]{:S(2)}, u32[]{:S(2)}) collective-permute-start(bf16[512,512]{1,0:T(8,128)(2,1)S(1)} %collective-permute-done.2.refs_6_.lower_ref), channel_id=1, source_target_pairs={{16,8},{20,12},{8,0},{12,4},{17,9},{21,13},{9,1},{13,5},{18,10},{2... | collective-permute-start | bytes 1572872 | tf_op jit(solution)/shard_map/ppermute | solution.py:511
  25.9 17.6 %collective-permute-start.6 = (bf16[512,512]{1,0:T(8,128)(2,1)S(1)}, bf16[512,512]{1,0:T(8,128)(2,1)S(1)}, u32[]{:S(2)}, u32[]{:S(2)}) collective-permute-start(bf16[512,512]{1,0:T(8,128)(2,1)S(1)} %pick.2), channel_id=1, source_target_pairs={{0,4},{4,0},{8,12},{12,8},{16,20},{20,16},{24,28},{28,24},{1,5},{5... | collective-permute-start | bytes 1572872 | tf_op jit(solution)/shard_map/ppermute | solution.py:511
  26.5 17.0 %collective-permute-start.7 = (bf16[512,512]{1,0:T(8,128)(2,1)}, bf16[512,512]{1,0:T(8,128)(2,1)S(1)}, u32[]{:S(2)}, u32[]{:S(2)}) collective-permute-start(bf16[512,512]{1,0:T(8,128)(2,1)} %collective-permute-done.3.refs_7_), channel_id=1, source_target_pairs={{0,8},{4,12},{24,16},{28,20},{1,9},{5,13},{25,17},{29,21},{2,10},{... | collective-permute-start | bytes 1572872 | tf_op jit(solution)/shard_map/ppermute | solution.py:511
  34.4 24.7 %copy-start.5 = (bf16[512,2560]{1,0:T(8,128)(2,1)S(1)}, bf16[512,2560]{1,0:T(8,128)(2,1)}, u32[]{:S(2)}) copy-start(bf16[512,2560]{1,0:T(8,128)(2,1)} %refs_12_.3) | copy-start | bytes 7864324
  41.2 11.0 %collective-permute-start.9 = (bf16[512,512]{1,0:T(8,128)(2,1)S(1)}, bf16[512,512]{1,0:T(8,128)(2,1)S(1)}, u32[]{:S(2)}, u32[]{:S(2)}) collective-permute-start(bf16[512,512]{1,0:T(8,128)(2,1)S(1)} %pick.3), channel_id=1, source_target_pairs={{0,4},{4,0},{8,12},{12,8},{16,20},{20,16},{24,28},{28,24},{1,5},{5... | collective-permute-start | bytes 1572872 | tf_op jit(solution)/shard_map/ppermute | solution.py:511
  41.8 12.9 %collective-permute-start.8 = (bf16[512,512]{1,0:T(8,128)(2,1)S(1)}, bf16[512,512]{1,0:T(8,128)(2,1)S(1)}, u32[]{:S(2)}, u32[]{:S(2)}) collective-permute-start(bf16[512,512]{1,0:T(8,128)(2,1)S(1)} %pick.3), channel_id=1, source_target_pairs={{16,24},{20,28},{8,0},{12,4},{17,25},{21,29},{9,1},{13,5},{18,26},... | collective-permute-start | bytes 1572872 | tf_op jit(solution)/shard_map/ppermute | solution.py:511
  43.5 34.4 %copy-start = (bf16[2560,2560]{1,0:T(8,128)(2,1)S(1)}, bf16[2560,2560]{1,0:T(8,128)(2,1)}, u32[]{:S(2)}) copy-start(bf16[2560,2560]{1,0:T(8,128)(2,1)} %refs_6_.3) | copy-start | bytes 39321604
  52.3 8.3 %collective-permute-start.11 = (bf16[256,512]{1,0:T(8,128)(2,1)S(1)}, bf16[256,512]{1,0:T(8,128)(2,1)S(1)}, u32[]{:S(2)}, u32[]{:S(2)}) collective-permute-start(bf16[256,512]{1,0:T(8,128)(2,1)S(1)} %slice.8), channel_id=1, source_target_pairs={{16,24},{20,28},{8,0},{12,4},{17,25},{21,29},{9,1},{13,5},{18,26},... | collective-permute-start | bytes 786440 | tf_op jit(solution)/shard_map/ppermute | solution.py:511
  54.8 8.7 %collective-permute-start.10 = (bf16[256,512]{1,0:T(8,128)(2,1)S(1)}, bf16[256,512]{1,0:T(8,128)(2,1)S(1)}, u32[]{:S(2)}, u32[]{:S(2)}) collective-permute-start(bf16[256,512]{1,0:T(8,128)(2,1)S(1)} %slice.6), channel_id=1, source_target_pairs={{0,4},{4,0},{24,28},{28,24},{1,5},{5,1},{25,29},{29,25},{2,6},{6,2... | collective-permute-start | bytes 786440 | tf_op jit(solution)/shard_map/ppermute | solution.py:511
  59.1 16.6 %collective-permute-start.17 = (bf16[512,2560]{1,0:T(8,128)(2,1)S(1)}, bf16[512,2560]{1,0:T(8,128)(2,1)S(1)}, u32[]{:S(2)}, u32[]{:S(2)}) collective-permute-start(bf16[512,2560]{1,0:T(8,128)(2,1)S(1)} %copy-done.5), channel_id=1, source_target_pairs={{0,1},{1,0},{2,3},{3,2},{4,5},{5,4},{6,7},{7,6},{8,9},{9,8},{10,11... | collective-permute-start | bytes 7864328 | tf_op jit(solution)/shard_map/ppermute | solution.py:514
  66.4 10.8 %copy-start.3 = (bf16[256,512]{1,0:T(8,128)(2,1)}, bf16[256,512]{1,0:T(8,128)(2,1)S(1)}, u32[]{:S(2)}) copy-start(bf16[256,512]{1,0:T(8,128)(2,1)S(1)} %get-tuple-element.78.refs_1_) | copy-start | bytes 786436
  66.4 30.8 %copy-start.2 = (bf16[256,512]{1,0:T(8,128)(2,1)}, bf16[256,512]{1,0:T(8,128)(2,1)S(1)}, u32[]{:S(2)}) copy-start(bf16[256,512]{1,0:T(8,128)(2,1)S(1)} %get-tuple-element.76.refs_1_) | copy-start | bytes 786436
  66.5 10.8 %collective-permute-start.16 = (bf16[512,2560]{1,0:T(8,128)(2,1)S(1)}, bf16[512,2560]{1,0:T(8,128)(2,1)S(1)}, u32[]{:S(2)}, u32[]{:S(2)}) collective-permute-start(bf16[512,2560]{1,0:T(8,128)(2,1)S(1)} %collective-permute-done.refs_7_), channel_id=1, source_target_pairs={{0,1},{1,0},{2,3},{3,2},{4,5},{5,4},{6,7},{7,6},{8,9},{9,8},{10,11... | collective-permute-start | bytes 7864328 | tf_op jit(solution)/shard_map/ppermute | solution.py:514
  66.5 8.7 %collective-permute-start.14 = (bf16[256,512]{1,0:T(8,128)(2,1)S(1)}, bf16[256,512]{1,0:T(8,128)(2,1)S(1)}, u32[]{:S(2)}, u32[]{:S(2)}) collective-permute-start(bf16[256,512]{1,0:T(8,128)(2,1)S(1)} %get-tuple-element.76.refs_1_), channel_id=1, source_target_pairs={{0,2},{1,3},{2,0},{3,1},{4,6},{5,7},{6,4},{7,5},{8,10},{9,11},{10,... | collective-permute-start | bytes 786440 | tf_op jit(solution)/shard_map/ppermute | solution.py:517
  67.1 8.7 %collective-permute-start.13 = (bf16[256,512]{1,0:T(8,128)(2,1)S(1)}, bf16[256,512]{1,0:T(8,128)(2,1)S(1)}, u32[]{:S(2)}, u32[]{:S(2)}) collective-permute-start(bf16[256,512]{1,0:T(8,128)(2,1)S(1)} %get-tuple-element.78.refs_1_), channel_id=1, source_target_pairs={{0,1},{1,0},{2,3},{3,2},{4,5},{5,4},{6,7},{7,6},{8,9},{9,8},{10,11... | collective-permute-start | bytes 786440 | tf_op jit(solution)/shard_map/ppermute | solution.py:514
  75.3 2.0 %copy-start.10 = (bf16[256,512]{1,0:T(8,128)(2,1)}, bf16[256,512]{1,0:T(8,128)(2,1)S(1)}, u32[]{:S(2)}) copy-start(bf16[256,512]{1,0:T(8,128)(2,1)S(1)} %collective-permute-done.14.refs_3_) | copy-start | bytes 786436
  75.3 1.5 %collective-permute-start.15 = (bf16[256,512]{1,0:T(8,128)(2,1)S(1)}, bf16[256,512]{1,0:T(8,128)(2,1)S(1)}, u32[]{:S(2)}, u32[]{:S(2)}) collective-permute-start(bf16[256,512]{1,0:T(8,128)(2,1)S(1)} %collective-permute-done.14.refs_3_), channel_id=1, source_target_pairs={{0,1},{1,0},{2,3},{3,2},{4,5},{5,4},{6,7},{7,6},{8,9},{9,8},{10,11... | collective-permute-start | bytes 786440 | tf_op jit(solution)/shard_map/ppermute | solution.py:514
  75.3 22.2 %collective-permute-start.20 = (bf16[256,512]{1,0:T(8,128)(2,1)S(1)}, bf16[256,512]{1,0:T(8,128)(2,1)S(1)}, u32[]{:S(2)}, u32[]{:S(2)}) collective-permute-start(bf16[256,512]{1,0:T(8,128)(2,1)S(1)} %get-tuple-element.78.refs_1_), channel_id=1, source_target_pairs={{0,2},{1,3},{2,0},{3,1},{4,6},{5,7},{6,4},{7,5},{8,10},{9,11},{10,... | collective-permute-start | bytes 786440 | tf_op jit(solution)/shard_map/ppermute | solution.py:517
  75.8 1.5 %copy-start.6 = (bf16[512,2560]{1,0:T(8,128)(2,1)}, bf16[512,2560]{1,0:T(8,128)(2,1)S(1)}, u32[]{:S(2)}) copy-start(bf16[512,2560]{1,0:T(8,128)(2,1)S(1)} %collective-permute-done.17.refs_13_) | copy-start | bytes 7864324
  75.8 1.6 %copy-start.11 = (bf16[256,512]{1,0:T(8,128)(2,1)}, bf16[256,512]{1,0:T(8,128)(2,1)S(1)}, u32[]{:S(2)}) copy-start(bf16[256,512]{1,0:T(8,128)(2,1)S(1)} %collective-permute-done.13.refs_2_) | copy-start | bytes 786436
  77.2 0.7 copy-start.12
  96.6 1.7 %collective-permute-start.18 = (bf16[64,2560]{1,0:T(8,128)(2,1)S(1)}, bf16[64,2560]{1,0:T(8,128)(2,1)S(1)}, u32[]{:S(2)}, u32[]{:S(2)}) collective-permute-start(bf16[64,2560]{1,0:T(8,128)(2,1)S(1)} %get-tuple-element.74), channel_id=1, source_target_pairs={{0,1},{1,0},{2,3},{3,2},{4,5},{5,4},{6,7},{7,6},{8,9},{9,8},{10,11... | collective-permute-start | bytes 983048 | tf_op jit(solution)/shard_map/ppermute | solution.py:514
  96.9 1.9 %collective-permute-start.19 = (bf16[64,2560]{1,0:T(8,128)(2,1)S(1)}, bf16[64,2560]{1,0:T(8,128)(2,1)S(1)}, u32[]{:S(2)}, u32[]{:S(2)}) collective-permute-start(bf16[64,2560]{1,0:T(8,128)(2,1)S(1)} %get-tuple-element.75), channel_id=1, source_target_pairs={{0,1},{1,0},{2,3},{3,2},{4,5},{5,4},{6,7},{7,6},{8,9},{9,8},{10,11... | collective-permute-start | bytes 983048 | tf_op jit(solution)/shard_map/ppermute | solution.py:514
  97.2 2.0 %collective-permute-start.12 = (bf16[256,512]{1,0:T(8,128)(2,1)S(1)}, bf16[256,512]{1,0:T(8,128)(2,1)S(1)}, u32[]{:S(2)}, u32[]{:S(2)}) collective-permute-start(bf16[256,512]{1,0:T(8,128)(2,1)S(1)} %get-tuple-element.76.refs_1_), channel_id=1, source_target_pairs={{0,1},{1,0},{2,3},{3,2},{4,5},{5,4},{6,7},{7,6},{8,9},{9,8},{10,11... | collective-permute-start | bytes 786440 | tf_op jit(solution)/shard_map/ppermute | solution.py:514
  97.5 3.3 %copy-start.7 = (bf16[256,512]{1,0:T(8,128)(2,1)}, bf16[256,512]{1,0:T(8,128)(2,1)S(1)}, u32[]{:S(2)}) copy-start(bf16[256,512]{1,0:T(8,128)(2,1)S(1)} %collective-permute-done.20.refs_3_) | copy-start | bytes 786436
  97.5 3.3 %collective-permute-start.21 = (bf16[256,512]{1,0:T(8,128)(2,1)S(1)}, bf16[256,512]{1,0:T(8,128)(2,1)S(1)}, u32[]{:S(2)}, u32[]{:S(2)}) collective-permute-start(bf16[256,512]{1,0:T(8,128)(2,1)S(1)} %collective-permute-done.20.refs_3_), channel_id=1, source_target_pairs={{0,1},{1,0},{2,3},{3,2},{4,5},{5,4},{6,7},{7,6},{8,9},{9,8},{10,11... | collective-permute-start | bytes 786440 | tf_op jit(solution)/shard_map/ppermute | solution.py:514
  99.2 1.5 %copy-start.8 = (bf16[256,512]{1,0:T(8,128)(2,1)}, bf16[256,512]{1,0:T(8,128)(2,1)S(1)}, u32[]{:S(2)}) copy-start(bf16[256,512]{1,0:T(8,128)(2,1)S(1)} %collective-permute-done.12.refs_2_) | copy-start | bytes 786436
  99.2 21.3 %collective-permute-start.22 = (bf16[128,2560]{1,0:T(8,128)(2,1)S(1)}, bf16[128,2560]{1,0:T(8,128)(2,1)S(1)}, u32[]{:S(2)}, u32[]{:S(2)}) collective-permute-start(bf16[128,2560]{1,0:T(8,128)(2,1)S(1)} %join.1), channel_id=1, source_target_pairs={{0,2},{1,3},{2,0},{3,1},{4,6},{5,7},{6,4},{7,5},{8,10},{9,11},{10,... | collective-permute-start | bytes 1966088 | tf_op jit(solution)/shard_map/ppermute | solution.py:517
  100.7 0.7 copy-start.9
  120.5 2.2 %copy-start.1 = (f32[3,2560]{1,0:T(4,128)S(1)}, f32[3,2560]{1,0:T(4,128)}, u32[]{:S(2)}) copy-start(f32[3,2560]{1,0:T(4,128)} %pad_maximum_fusion.1.refs_5_.refs_2_) | copy-start | bytes 92164
  120.5 1.7 %collective-permute-start.23 = (bf16[64,2560]{1,0:T(8,128)(2,1)S(1)}, bf16[64,2560]{1,0:T(8,128)(2,1)S(1)}, u32[]{:S(2)}, u32[]{:S(2)}) collective-permute-start(bf16[64,2560]{1,0:T(8,128)(2,1)S(1)} %get-tuple-element.85), channel_id=1, source_target_pairs={{0,1},{1,0},{2,3},{3,2},{4,5},{5,4},{6,7},{7,6},{8,9},{9,8},{10,11... | collective-permute-start | bytes 983048 | tf_op jit(solution)/shard_map/ppermute | solution.py:514
  120.6 2.1 %collective-permute-start.24 = (bf16[64,2560]{1,0:T(8,128)(2,1)S(1)}, bf16[64,2560]{1,0:T(8,128)(2,1)S(1)}, u32[]{:S(2)}, u32[]{:S(2)}) collective-permute-start(bf16[64,2560]{1,0:T(8,128)(2,1)S(1)} %get-tuple-element.86), channel_id=1, source_target_pairs={{0,1},{1,0},{2,3},{3,2},{4,5},{5,4},{6,7},{7,6},{8,9},{9,8},{10,11... | collective-permute-start | bytes 983048 | tf_op jit(solution)/shard_map/ppermute | solution.py:514

commit v2 on v1

--- a/solution.py
+++ b/solution.py
@@ -315,7 +315,7 @@
         copy.start()
     wide = column_step(width)
 
-    @pl.loop(0, width // wide)
+    @pl.loop(0, width // wide, unroll=5)
     def _(at):
         columns = columns_of(at, wide)
         total = jnp.dot(heads_refs[2][...], weight_refs[0][:, columns], preferred_element_type=F32)
@@ -328,7 +328,7 @@
     for copy in near_copies:
         copy.wait()
 
-    @pl.loop(0, width // wide)
+    @pl.loop(0, width // wide, unroll=5)
     def _(at):
         columns = columns_of(at, wide)
         total = total_ref[:, columns]

time: 125 us -> 122 us (0.976)
  waiting for transfers between devices: 26.2 us -> 23.3 us
    ppermute x11, waiting for transfers between devices: 14.4 us -> 11.4 us  [move(): return lax.ppermute(values_in, 'req', pairs)]
    pallas_call x2, Pallas kernels: 37.7 us -> 36.4 us  [feed_rows(): pl.pallas_call(functools.partial(feed_kernel, pieces, group, planes), in_...]
  transfers between devices with their start and end apart: 25 -> 25, of which waited for: 14 -> 14; matrix products, arithmetic and copies ran while one was open for 3% -> 4% of each run, Pallas kernels for 44% -> 45%
where the time goes in v2:
time: 122 us; the launch traced here: 121 us
  Pallas kernels  55.6 us (46%)
  starting transfers between devices  33.6 us (28%)
  waiting for transfers between devices  23.3 us (19%)
  local copies, waits for them, and re-layouts  5.89 us (5%)
  other arithmetic  2.17 us (2%)
    pallas_call x2, Pallas kernels, feed_rows(): pl.pallas_call(functools.partial(feed_kernel, pieces, group, planes), in_...  36.4 us
    ppermute x11, starting transfers between devices, move(): return lax.ppermute(values_in, 'req', pairs)  26.1 us
    pallas_call x5, Pallas kernels, attention_call(): pl.pallas_call(kernel, in_specs=in_specs, out_specs=[VMEM] * len(out_shap...  15.9 us
    ppermute x11, waiting for transfers between devices, move(): return lax.ppermute(values_in, 'req', pairs)  11.4 us
    ppermute x4, waiting for transfers between devices, plane_shift(): lax.ppermute(values_in, 'tok', [(at, (at + CORES * shift) % tok_count) fo...  7.99 us
    ppermute x4, starting transfers between devices, plane_shift(): lax.ppermute(values_in, 'tok', [(at, (at + CORES * shift) % tok_count) fo...  5.57 us
    ppermute x10, waiting for transfers between devices, other_core(): lax.ppermute(values_in, 'tok', [(at, at ^ 1) for at in range(tok_count)])  3.82 us
  transfers between devices with their start and end apart: 25, of which 14 were waited for; matrix products, arithmetic and copies ran while one was open for 4% of the time, Pallas kernels for 45%

profile of v2, /device:TPU:0, one launch (start us, length us, event | category | flops | bytes accessed | tf_op | source)
XLA Modules:
  0.0 120.9 jit_solution(2100185574466312374)
XLA Ops:
  0.0 1.1 constant_dynamic-slice_fusion.1
  1.1 0.8 pad_maximum_fusion.refs_4_
  1.9 3.0 %collective-permute-start = (bf16[512,2560]{1,0:T(8,128)(2,1)}, bf16[512,2560]{1,0:T(8,128)(2,1)S(1)}, u32[]{:S(2)}, u32[]{:S(2)}) collective-permute-start(bf16[512,2560]{1,0:T(8,128)(2,1)} %refs_12_.3), channel_id=1, source_target_pairs={{0,2},{1,3},{2,0},{3,1},{4,6},{5,7},{6,4},{7,5},{8,10},{9,11},{10,... | collective-permute-start | bytes 7864328 | tf_op jit(solution)/shard_map/ppermute | solution.py:517
  4.9 1.5 %collective-permute-start.3 = (bf16[512,512]{1,0:T(8,128)(2,1)}, bf16[512,512]{1,0:T(8,128)(2,1)}, u32[]{:S(2)}, u32[]{:S(2)}) collective-permute-start(bf16[512,512]{1,0:T(8,128)(2,1)} %pad_maximum_fusion.refs_4_), channel_id=1, source_target_pairs={{0,4},{4,0},{8,12},{12,8},{16,20},{20,16},{24,28},{28,24},{1,5},{5... | collective-permute-start | bytes 1572872 | tf_op jit(solution)/shard_map/ppermute | solution.py:511
  6.4 1.3 %collective-permute-start.2 = (bf16[512,512]{1,0:T(8,128)(2,1)}, bf16[512,512]{1,0:T(8,128)(2,1)S(1)}, u32[]{:S(2)}, u32[]{:S(2)}) collective-permute-start(bf16[512,512]{1,0:T(8,128)(2,1)} %pad_maximum_fusion.refs_4_), channel_id=1, source_target_pairs={{8,0},{12,4},{16,8},{20,12},{24,16},{28,20},{9,1},{13,5},{17,9},{2... | collective-permute-start | bytes 1572872 | tf_op jit(solution)/shard_map/ppermute | solution.py:511
  7.7 5.4 %collective-permute-start.1 = (bf16[512,512]{1,0:T(8,128)(2,1)}, bf16[512,512]{1,0:T(8,128)(2,1)}, u32[]{:S(2)}, u32[]{:S(2)}) collective-permute-start(bf16[512,512]{1,0:T(8,128)(2,1)} %pad_maximum_fusion.refs_4_), channel_id=1, source_target_pairs={{0,8},{4,12},{8,16},{12,20},{16,24},{20,28},{1,9},{5,13},{9,17},{1... | collective-permute-start | bytes 1572872 | tf_op jit(solution)/shard_map/ppermute | solution.py:511
  13.0 0.7 stack.33
  13.8 0.7 stack.34
  14.5 0.7 stack.35
  15.2 0.8 concatenate.6.refs_0_.numbers
  15.9 0.6 pad_maximum_fusion.1.refs_5_.refs_2_
  16.6 0.7 pad_maximum_fusion.2.refs_3_
  17.3 3.4 %attend_blocks.5 = (bf16[512,512]{1,0:T(8,128)(2,1)S(1)}, f32[2,512,128]{2,1,0:T(8,128)S(1)}, f32[2,512,128]{2,1,0:T(8,128)S(1)}, f32[512,512]{1,0:T(8,128)S(1)}) custom-call(s32[22]{0:T(128)S(1)} %concatenate.6.refs_0_.numbers, bf16[512,512]{1,0:T(8,128)(2,1)} %refs_1_.1, bf16[512,2048]{1,0:T(8,128)(2,1)} %refs_2_.1, ...), custom_call_target="tpu_custom_call" | custom-call | flops 1073741824 | bytes 4194304 | tf_op jit(solution)/shard_map/attend_blocks/pallas_call | solution.py:227
  20.7 0.9 collective-permute-done.2.refs_6_.lower_ref
  21.6 1.3 %collective-permute-done.1.refs_5_.upper_ref = bf16[512,512]{1,0:T(8,128)(2,1)} collective-permute-done((bf16[512,512]{1,0:T(8,128)(2,1)}, bf16[512,512]{1,0:T(8,128)(2,1)}, u32[]{:S(2)}, u32[]{:S(2)}) %collective-permute-start.1) | collective-permute-done | bytes 524320 | tf_op jit(solution)/shard_map/ppermute | solution.py:511
  22.8 0.7 collective-permute-start.4
  23.5 1.3 %collective-permute-start.5 = (bf16[512,512]{1,0:T(8,128)(2,1)S(1)}, bf16[512,512]{1,0:T(8,128)(2,1)S(1)}, u32[]{:S(2)}, u32[]{:S(2)}) collective-permute-start(bf16[512,512]{1,0:T(8,128)(2,1)S(1)} %collective-permute-done.2.refs_6_.lower_ref), channel_id=1, source_target_pairs={{16,8},{20,12},{8,0},{12,4},{17,9},{21,13},{9,1},{13,5},{18,10},{2... | collective-permute-start | bytes 1572872 | tf_op jit(solution)/shard_map/ppermute | solution.py:511
  24.8 1.1 pick.2
  25.9 0.6 collective-permute-start.6
  26.5 7.9 %collective-permute-start.7 = (bf16[512,512]{1,0:T(8,128)(2,1)}, bf16[512,512]{1,0:T(8,128)(2,1)S(1)}, u32[]{:S(2)}, u32[]{:S(2)}) collective-permute-start(bf16[512,512]{1,0:T(8,128)(2,1)} %collective-permute-done.3.refs_7_), channel_id=1, source_target_pairs={{0,8},{4,12},{24,16},{28,20},{1,9},{5,13},{25,17},{29,21},{2,10},{... | collective-permute-start | bytes 1572872 | tf_op jit(solution)/shard_map/ppermute | solution.py:511
  34.4 3.9 %attend_blocks.6 = (f32[2,512,128]{2,1,0:T(8,128)S(1)}, f32[2,512,128]{2,1,0:T(8,128)S(1)}, f32[512,512]{1,0:T(8,128)S(1)}) custom-call(s32[22]{0:T(128)S(1)} %concatenate.6.refs_0_.numbers, bf16[512,512]{1,0:T(8,128)(2,1)S(1)} %get-tuple-element.49.refs_1_, f32[2,512,128]{2,1,0:T(8,128)S(1)} %get-tuple-element.50.refs_2_, ...), custom_call_target="tpu_custom_call" | custom-call | flops 1073741824 | bytes 4194304 | tf_op jit(solution)/shard_map/attend_blocks/pallas_call | solution.py:227
  38.3 2.3 %collective-permute-done.5.refs_6_.lower_ref = bf16[512,512]{1,0:T(8,128)(2,1)S(1)} collective-permute-done((bf16[512,512]{1,0:T(8,128)(2,1)S(1)}, bf16[512,512]{1,0:T(8,128)(2,1)S(1)}, u32[]{:S(2)}, u32[]{:S(2)}) %collective-permute-start.5) | collective-permute-done | bytes 524320 | tf_op jit(solution)/shard_map/ppermute | solution.py:511
  40.6 0.6 pick.3
  41.2 0.6 collective-permute-start.9
  41.8 1.3 %collective-permute-start.8 = (bf16[512,512]{1,0:T(8,128)(2,1)S(1)}, bf16[512,512]{1,0:T(8,128)(2,1)S(1)}, u32[]{:S(2)}, u32[]{:S(2)}) collective-permute-start(bf16[512,512]{1,0:T(8,128)(2,1)S(1)} %pick.3), channel_id=1, source_target_pairs={{16,24},{20,28},{8,0},{12,4},{17,25},{21,29},{9,1},{13,5},{18,26},... | collective-permute-start | bytes 1572872 | tf_op jit(solution)/shard_map/ppermute | solution.py:511
  43.5 4.8 %attend_blocks.7 = (f32[2,512,128]{2,1,0:T(8,128)S(1)}, f32[2,512,128]{2,1,0:T(8,128)S(1)}, f32[512,512]{1,0:T(8,128)S(1)}) custom-call(s32[22]{0:T(128)S(1)} %concatenate.6.refs_0_.numbers, bf16[512,512]{1,0:T(8,128)(2,1)S(1)} %get-tuple-element.49.refs_1_, f32[2,512,128]{2,1,0:T(8,128)S(1)} %get-tuple-element.53.refs_2_, ...), custom_call_target="tpu_custom_call" | custom-call | flops 1073741824 | bytes 4194304 | tf_op jit(solution)/shard_map/attend_blocks/pallas_call | solution.py:227
  48.4 3.9 %collective-permute-done.9.refs_6_ = bf16[512,512]{1,0:T(8,128)(2,1)S(1)} collective-permute-done((bf16[512,512]{1,0:T(8,128)(2,1)S(1)}, bf16[512,512]{1,0:T(8,128)(2,1)S(1)}, u32[]{:S(2)}, u32[]{:S(2)}) %collective-permute-start.9) | collective-permute-done | bytes 524320 | tf_op jit(solution)/shard_map/ppermute | solution.py:511
  52.3 1.3 %collective-permute-start.11 = (bf16[256,512]{1,0:T(8,128)(2,1)S(1)}, bf16[256,512]{1,0:T(8,128)(2,1)S(1)}, u32[]{:S(2)}, u32[]{:S(2)}) collective-permute-start(bf16[256,512]{1,0:T(8,128)(2,1)S(1)} %slice.8), channel_id=1, source_target_pairs={{16,24},{20,28},{8,0},{12,4},{17,25},{21,29},{9,1},{13,5},{18,26},... | collective-permute-start | bytes 786440 | tf_op jit(solution)/shard_map/ppermute | solution.py:511
  53.6 1.2 collective-permute-done.8.refs_5_
  54.8 4.4 %collective-permute-start.10 = (bf16[256,512]{1,0:T(8,128)(2,1)S(1)}, bf16[256,512]{1,0:T(8,128)(2,1)S(1)}, u32[]{:S(2)}, u32[]{:S(2)}) collective-permute-start(bf16[256,512]{1,0:T(8,128)(2,1)S(1)} %slice.6), channel_id=1, source_target_pairs={{0,4},{4,0},{24,28},{28,24},{1,5},{5,1},{25,29},{29,25},{2,6},{6,2... | collective-permute-start | bytes 786440 | tf_op jit(solution)/shard_map/ppermute | solution.py:511
  59.2 2.8 %attend_blocks.8 = (f32[2,512,128]{2,1,0:T(8,128)S(1)}, f32[2,512,128]{2,1,0:T(8,128)S(1)}, f32[512,512]{1,0:T(8,128)S(1)}) custom-call(s32[22]{0:T(128)S(1)} %concatenate.6.refs_0_.numbers, bf16[512,512]{1,0:T(8,128)(2,1)S(1)} %get-tuple-element.49.refs_1_, f32[2,512,128]{2,1,0:T(8,128)S(1)} %get-tuple-element.58.refs_2_, ...), custom_call_target="tpu_custom_call" | custom-call | flops 1073741824 | bytes 4194304 | tf_op jit(solution)/shard_map/attend_blocks/pallas_call | solution.py:227
  62.0 1.5 %collective-permute-done.10.refs_5_ = bf16[256,512]{1,0:T(8,128)(2,1)S(1)} collective-permute-done((bf16[256,512]{1,0:T(8,128)(2,1)S(1)}, bf16[256,512]{1,0:T(8,128)(2,1)S(1)}, u32[]{:S(2)}, u32[]{:S(2)}) %collective-permute-start.10) | collective-permute-done | bytes 262176 | tf_op jit(solution)/shard_map/ppermute | solution.py:511
  63.5 1.1 attend_blocks.9
  64.7 0.6 collective-permute-start.14
  65.4 8.0 %collective-permute-done.14.refs_3_ = bf16[256,512]{1,0:T(8,128)(2,1)S(1)} collective-permute-done((bf16[256,512]{1,0:T(8,128)(2,1)S(1)}, bf16[256,512]{1,0:T(8,128)(2,1)S(1)}, u32[]{:S(2)}, u32[]{:S(2)}) %collective-permute-start.14) | collective-permute-done | bytes 262176 | tf_op jit(solution)/shard_map/ppermute | solution.py:517
  73.4 0.5 collective-permute-start.20
  74.0 1.0 collective-permute-done.15.refs_4_
  75.5 0.6 copy-done.12
  76.1 18.0 %feed_rows.2 = (f32[128,2560]{1,0:T(8,128)S(1)}, bf16[64,2560]{1,0:T(8,128)(2,1)S(1)}, bf16[64,2560]{1,0:T(8,128)(2,1)S(1)}) custom-call(s32[22]{0:T(128)} %copy-done.4, bf16[256,512]{1,0:T(8,128)(2,1)} %copy-done.3, bf16[256,512]{1,0:T(8,128)(2,1)} %copy-done.11, bf16[256,512]{1,0:T(8,128)(2,1)} %copy-done.10, bf16[256,512]{1,0:T(8,128)(2,1)} %copy-done.12, ...), custom_call_target="tpu_custom_call" | custom-call | flops 12750684160 | bytes 16777216 | tf_op jit(solution)/shard_map/feed_rows/pallas_call | solution.py:389
  95.3 0.6 collective-permute-done.18.refs_0_
  95.9 0.5 collective-permute-done.19.refs_1_
  96.7 1.5 %collective-permute-start.22 = (bf16[128,2560]{1,0:T(8,128)(2,1)S(1)}, bf16[128,2560]{1,0:T(8,128)(2,1)S(1)}, u32[]{:S(2)}, u32[]{:S(2)}) collective-permute-start(bf16[128,2560]{1,0:T(8,128)(2,1)S(1)} %join.1), channel_id=1, source_target_pairs={{0,2},{1,3},{2,0},{3,1},{4,6},{5,7},{6,4},{7,5},{8,10},{9,11},{10,... | collective-permute-start | bytes 1966088 | tf_op jit(solution)/shard_map/ppermute | solution.py:517
  98.2 0.7 copy-done.9
  99.0 18.4 %feed_rows.3 = (f32[128,2560]{1,0:T(8,128)S(1)}, bf16[64,2560]{1,0:T(8,128)(2,1)S(1)}, bf16[64,2560]{1,0:T(8,128)(2,1)S(1)}, f32[128,2560]{1,0:T(8,128)S(1)}) custom-call(s32[22]{0:T(128)} %copy-done.4, bf16[256,512]{1,0:T(8,128)(2,1)} %copy-done.2, bf16[256,512]{1,0:T(8,128)(2,1)} %copy-done.8, bf16[256,512]{1,0:T(8,128)(2,1)} %copy-done.7, ...), custom_call_target="tpu_custom_call" | custom-call | flops 12750684160 | bytes 16777216 | tf_op jit(solution)/shard_map/feed_rows/pallas_call | solution.py:389
  117.4 0.5 collective-permute-start.24
  118.1 1.0 collective-permute-done.23.refs_0_
  119.1 0.5 collective-permute-done.24.refs_1_
  119.5 1.3 %finish.1 = bf16[128,2560]{1,0:T(8,128)(2,1)} custom-call(f32[128,2560]{1,0:T(8,128)S(1)} %get-tuple-element.79.mixed_ref, f32[128,2560]{1,0:T(8,128)S(1)} %fold.1.total_ref, bf16[64,2560]{1,0:T(8,128)(2,1)S(1)} %collective-permute-done.23.refs_0_, bf16[64,2560]{1,0:T(8,128)(2,1)S(1)} %collective-permute-done.24.refs_1_, f32[3,2560]{1,0:T(4,128)S(1)} %copy-done.1), custom_call_target="tpu_custom_call" | custom-call | tf_op jit(solution)/shard_map/finish/pallas_call | solution.py:463
  (50 shorter events, 3.0 us)
Async XLA Ops:
  1.9 62.7 %collective-permute-start = (bf16[512,2560]{1,0:T(8,128)(2,1)}, bf16[512,2560]{1,0:T(8,128)(2,1)S(1)}, u32[]{:S(2)}, u32[]{:S(2)}) collective-permute-start(bf16[512,2560]{1,0:T(8,128)(2,1)} %refs_12_.3), channel_id=1, source_target_pairs={{0,2},{1,3},{2,0},{3,1},{4,6},{5,7},{6,4},{7,5},{8,10},{9,11},{10,... | collective-permute-start | bytes 7864328 | tf_op jit(solution)/shard_map/ppermute | solution.py:517
  4.9 21.7 %collective-permute-start.3 = (bf16[512,512]{1,0:T(8,128)(2,1)}, bf16[512,512]{1,0:T(8,128)(2,1)}, u32[]{:S(2)}, u32[]{:S(2)}) collective-permute-start(bf16[512,512]{1,0:T(8,128)(2,1)} %pad_maximum_fusion.refs_4_), channel_id=1, source_target_pairs={{0,4},{4,0},{8,12},{12,8},{16,20},{20,16},{24,28},{28,24},{1,5},{5... | collective-permute-start | bytes 1572872 | tf_op jit(solution)/shard_map/ppermute | solution.py:511
  6.4 15.2 %collective-permute-start.2 = (bf16[512,512]{1,0:T(8,128)(2,1)}, bf16[512,512]{1,0:T(8,128)(2,1)S(1)}, u32[]{:S(2)}, u32[]{:S(2)}) collective-permute-start(bf16[512,512]{1,0:T(8,128)(2,1)} %pad_maximum_fusion.refs_4_), channel_id=1, source_target_pairs={{8,0},{12,4},{16,8},{20,12},{24,16},{28,20},{9,1},{13,5},{17,9},{2... | collective-permute-start | bytes 1572872 | tf_op jit(solution)/shard_map/ppermute | solution.py:511
  7.7 15.2 %collective-permute-start.1 = (bf16[512,512]{1,0:T(8,128)(2,1)}, bf16[512,512]{1,0:T(8,128)(2,1)}, u32[]{:S(2)}, u32[]{:S(2)}) collective-permute-start(bf16[512,512]{1,0:T(8,128)(2,1)} %pad_maximum_fusion.refs_4_), channel_id=1, source_target_pairs={{0,8},{4,12},{8,16},{12,20},{16,24},{20,28},{1,9},{5,13},{9,17},{1... | collective-permute-start | bytes 1572872 | tf_op jit(solution)/shard_map/ppermute | solution.py:511
  15.9 47.5 %copy-start.4 = (s32[22]{0:T(128)}, s32[22]{0:T(128)S(1)}, u32[]{:S(2)}) copy-start(s32[22]{0:T(128)S(1)} %concatenate.6.refs_0_.numbers) | copy-start | bytes 268
  22.8 15.4 %collective-permute-start.4 = (bf16[512,512]{1,0:T(8,128)(2,1)}, bf16[512,512]{1,0:T(8,128)(2,1)S(1)}, u32[]{:S(2)}, u32[]{:S(2)}) collective-permute-start(bf16[512,512]{1,0:T(8,128)(2,1)} %collective-permute-done.1.refs_5_.upper_ref), channel_id=1, source_target_pairs={{8,16},{12,20},{16,24},{20,28},{9,17},{13,21},{17,25},{21,29},{10,... | collective-permute-start | bytes 1572872 | tf_op jit(solution)/shard_map/ppermute | solution.py:511
  23.5 17.1 %collective-permute-start.5 = (bf16[512,512]{1,0:T(8,128)(2,1)S(1)}, bf16[512,512]{1,0:T(8,128)(2,1)S(1)}, u32[]{:S(2)}, u32[]{:S(2)}) collective-permute-start(bf16[512,512]{1,0:T(8,128)(2,1)S(1)} %collective-permute-done.2.refs_6_.lower_ref), channel_id=1, source_target_pairs={{16,8},{20,12},{8,0},{12,4},{17,9},{21,13},{9,1},{13,5},{18,10},{2... | collective-permute-start | bytes 1572872 | tf_op jit(solution)/shard_map/ppermute | solution.py:511
  25.9 17.6 %collective-permute-start.6 = (bf16[512,512]{1,0:T(8,128)(2,1)S(1)}, bf16[512,512]{1,0:T(8,128)(2,1)S(1)}, u32[]{:S(2)}, u32[]{:S(2)}) collective-permute-start(bf16[512,512]{1,0:T(8,128)(2,1)S(1)} %pick.2), channel_id=1, source_target_pairs={{0,4},{4,0},{8,12},{12,8},{16,20},{20,16},{24,28},{28,24},{1,5},{5... | collective-permute-start | bytes 1572872 | tf_op jit(solution)/shard_map/ppermute | solution.py:511
  26.5 17.0 %collective-permute-start.7 = (bf16[512,512]{1,0:T(8,128)(2,1)}, bf16[512,512]{1,0:T(8,128)(2,1)S(1)}, u32[]{:S(2)}, u32[]{:S(2)}) collective-permute-start(bf16[512,512]{1,0:T(8,128)(2,1)} %collective-permute-done.3.refs_7_), channel_id=1, source_target_pairs={{0,8},{4,12},{24,16},{28,20},{1,9},{5,13},{25,17},{29,21},{2,10},{... | collective-permute-start | bytes 1572872 | tf_op jit(solution)/shard_map/ppermute | solution.py:511
  34.4 24.7 %copy-start.5 = (bf16[512,2560]{1,0:T(8,128)(2,1)S(1)}, bf16[512,2560]{1,0:T(8,128)(2,1)}, u32[]{:S(2)}) copy-start(bf16[512,2560]{1,0:T(8,128)(2,1)} %refs_12_.3) | copy-start | bytes 7864324
  41.2 11.0 %collective-permute-start.9 = (bf16[512,512]{1,0:T(8,128)(2,1)S(1)}, bf16[512,512]{1,0:T(8,128)(2,1)S(1)}, u32[]{:S(2)}, u32[]{:S(2)}) collective-permute-start(bf16[512,512]{1,0:T(8,128)(2,1)S(1)} %pick.3), channel_id=1, source_target_pairs={{0,4},{4,0},{8,12},{12,8},{16,20},{20,16},{24,28},{28,24},{1,5},{5... | collective-permute-start | bytes 1572872 | tf_op jit(solution)/shard_map/ppermute | solution.py:511
  41.8 12.9 %collective-permute-start.8 = (bf16[512,512]{1,0:T(8,128)(2,1)S(1)}, bf16[512,512]{1,0:T(8,128)(2,1)S(1)}, u32[]{:S(2)}, u32[]{:S(2)}) collective-permute-start(bf16[512,512]{1,0:T(8,128)(2,1)S(1)} %pick.3), channel_id=1, source_target_pairs={{16,24},{20,28},{8,0},{12,4},{17,25},{21,29},{9,1},{13,5},{18,26},... | collective-permute-start | bytes 1572872 | tf_op jit(solution)/shard_map/ppermute | solution.py:511
  43.5 32.6 %copy-start = (bf16[2560,2560]{1,0:T(8,128)(2,1)S(1)}, bf16[2560,2560]{1,0:T(8,128)(2,1)}, u32[]{:S(2)}) copy-start(bf16[2560,2560]{1,0:T(8,128)(2,1)} %refs_6_.3) | copy-start | bytes 39321604
  52.3 9.7 %collective-permute-start.11 = (bf16[256,512]{1,0:T(8,128)(2,1)S(1)}, bf16[256,512]{1,0:T(8,128)(2,1)S(1)}, u32[]{:S(2)}, u32[]{:S(2)}) collective-permute-start(bf16[256,512]{1,0:T(8,128)(2,1)S(1)} %slice.8), channel_id=1, source_target_pairs={{16,24},{20,28},{8,0},{12,4},{17,25},{21,29},{9,1},{13,5},{18,26},... | collective-permute-start | bytes 786440 | tf_op jit(solution)/shard_map/ppermute | solution.py:511
  54.8 8.7 %collective-permute-start.10 = (bf16[256,512]{1,0:T(8,128)(2,1)S(1)}, bf16[256,512]{1,0:T(8,128)(2,1)S(1)}, u32[]{:S(2)}, u32[]{:S(2)}) collective-permute-start(bf16[256,512]{1,0:T(8,128)(2,1)S(1)} %slice.6), channel_id=1, source_target_pairs={{0,4},{4,0},{24,28},{28,24},{1,5},{5,1},{25,29},{29,25},{2,6},{6,2... | collective-permute-start | bytes 786440 | tf_op jit(solution)/shard_map/ppermute | solution.py:511
  59.1 14.8 %collective-permute-start.17 = (bf16[512,2560]{1,0:T(8,128)(2,1)S(1)}, bf16[512,2560]{1,0:T(8,128)(2,1)S(1)}, u32[]{:S(2)}, u32[]{:S(2)}) collective-permute-start(bf16[512,2560]{1,0:T(8,128)(2,1)S(1)} %copy-done.5), channel_id=1, source_target_pairs={{0,1},{1,0},{2,3},{3,2},{4,5},{5,4},{6,7},{7,6},{8,9},{9,8},{10,11... | collective-permute-start | bytes 7864328 | tf_op jit(solution)/shard_map/ppermute | solution.py:514
  64.6 10.8 %copy-start.3 = (bf16[256,512]{1,0:T(8,128)(2,1)}, bf16[256,512]{1,0:T(8,128)(2,1)S(1)}, u32[]{:S(2)}) copy-start(bf16[256,512]{1,0:T(8,128)(2,1)S(1)} %get-tuple-element.78.refs_1_) | copy-start | bytes 786436
  64.6 30.1 %copy-start.2 = (bf16[256,512]{1,0:T(8,128)(2,1)}, bf16[256,512]{1,0:T(8,128)(2,1)S(1)}, u32[]{:S(2)}) copy-start(bf16[256,512]{1,0:T(8,128)(2,1)S(1)} %get-tuple-element.76.refs_1_) | copy-start | bytes 786436
  64.6 10.8 %collective-permute-start.16 = (bf16[512,2560]{1,0:T(8,128)(2,1)S(1)}, bf16[512,2560]{1,0:T(8,128)(2,1)S(1)}, u32[]{:S(2)}, u32[]{:S(2)}) collective-permute-start(bf16[512,2560]{1,0:T(8,128)(2,1)S(1)} %collective-permute-done.refs_7_), channel_id=1, source_target_pairs={{0,1},{1,0},{2,3},{3,2},{4,5},{5,4},{6,7},{7,6},{8,9},{9,8},{10,11... | collective-permute-start | bytes 7864328 | tf_op jit(solution)/shard_map/ppermute | solution.py:514
  64.7 8.7 %collective-permute-start.14 = (bf16[256,512]{1,0:T(8,128)(2,1)S(1)}, bf16[256,512]{1,0:T(8,128)(2,1)S(1)}, u32[]{:S(2)}, u32[]{:S(2)}) collective-permute-start(bf16[256,512]{1,0:T(8,128)(2,1)S(1)} %get-tuple-element.76.refs_1_), channel_id=1, source_target_pairs={{0,2},{1,3},{2,0},{3,1},{4,6},{5,7},{6,4},{7,5},{8,10},{9,11},{10,... | collective-permute-start | bytes 786440 | tf_op jit(solution)/shard_map/ppermute | solution.py:517
  65.3 8.7 %collective-permute-start.13 = (bf16[256,512]{1,0:T(8,128)(2,1)S(1)}, bf16[256,512]{1,0:T(8,128)(2,1)S(1)}, u32[]{:S(2)}, u32[]{:S(2)}) collective-permute-start(bf16[256,512]{1,0:T(8,128)(2,1)S(1)} %get-tuple-element.78.refs_1_), channel_id=1, source_target_pairs={{0,1},{1,0},{2,3},{3,2},{4,5},{5,4},{6,7},{7,6},{8,9},{9,8},{10,11... | collective-permute-start | bytes 786440 | tf_op jit(solution)/shard_map/ppermute | solution.py:514
  73.4 2.0 %copy-start.10 = (bf16[256,512]{1,0:T(8,128)(2,1)}, bf16[256,512]{1,0:T(8,128)(2,1)S(1)}, u32[]{:S(2)}) copy-start(bf16[256,512]{1,0:T(8,128)(2,1)S(1)} %collective-permute-done.14.refs_3_) | copy-start | bytes 786436
  73.4 1.5 %collective-permute-start.15 = (bf16[256,512]{1,0:T(8,128)(2,1)S(1)}, bf16[256,512]{1,0:T(8,128)(2,1)S(1)}, u32[]{:S(2)}, u32[]{:S(2)}) collective-permute-start(bf16[256,512]{1,0:T(8,128)(2,1)S(1)} %collective-permute-done.14.refs_3_), channel_id=1, source_target_pairs={{0,1},{1,0},{2,3},{3,2},{4,5},{5,4},{6,7},{7,6},{8,9},{9,8},{10,11... | collective-permute-start | bytes 786440 | tf_op jit(solution)/shard_map/ppermute | solution.py:514
  73.4 21.5 %collective-permute-start.20 = (bf16[256,512]{1,0:T(8,128)(2,1)S(1)}, bf16[256,512]{1,0:T(8,128)(2,1)S(1)}, u32[]{:S(2)}, u32[]{:S(2)}) collective-permute-start(bf16[256,512]{1,0:T(8,128)(2,1)S(1)} %get-tuple-element.78.refs_1_), channel_id=1, source_target_pairs={{0,2},{1,3},{2,0},{3,1},{4,6},{5,7},{6,4},{7,5},{8,10},{9,11},{10,... | collective-permute-start | bytes 786440 | tf_op jit(solution)/shard_map/ppermute | solution.py:517
  73.9 1.5 %copy-start.6 = (bf16[512,2560]{1,0:T(8,128)(2,1)}, bf16[512,2560]{1,0:T(8,128)(2,1)S(1)}, u32[]{:S(2)}) copy-start(bf16[512,2560]{1,0:T(8,128)(2,1)S(1)} %collective-permute-done.17.refs_13_) | copy-start | bytes 7864324
  73.9 1.6 %copy-start.11 = (bf16[256,512]{1,0:T(8,128)(2,1)}, bf16[256,512]{1,0:T(8,128)(2,1)S(1)}, u32[]{:S(2)}) copy-start(bf16[256,512]{1,0:T(8,128)(2,1)S(1)} %collective-permute-done.13.refs_2_) | copy-start | bytes 786436
  75.4 0.7 copy-start.12
  94.2 1.7 %collective-permute-start.18 = (bf16[64,2560]{1,0:T(8,128)(2,1)S(1)}, bf16[64,2560]{1,0:T(8,128)(2,1)S(1)}, u32[]{:S(2)}, u32[]{:S(2)}) collective-permute-start(bf16[64,2560]{1,0:T(8,128)(2,1)S(1)} %get-tuple-element.74), channel_id=1, source_target_pairs={{0,1},{1,0},{2,3},{3,2},{4,5},{5,4},{6,7},{7,6},{8,9},{9,8},{10,11... | collective-permute-start | bytes 983048 | tf_op jit(solution)/shard_map/ppermute | solution.py:514
  94.5 1.9 %collective-permute-start.19 = (bf16[64,2560]{1,0:T(8,128)(2,1)S(1)}, bf16[64,2560]{1,0:T(8,128)(2,1)S(1)}, u32[]{:S(2)}, u32[]{:S(2)}) collective-permute-start(bf16[64,2560]{1,0:T(8,128)(2,1)S(1)} %get-tuple-element.75), channel_id=1, source_target_pairs={{0,1},{1,0},{2,3},{3,2},{4,5},{5,4},{6,7},{7,6},{8,9},{9,8},{10,11... | collective-permute-start | bytes 983048 | tf_op jit(solution)/shard_map/ppermute | solution.py:514
  94.7 2.0 %collective-permute-start.12 = (bf16[256,512]{1,0:T(8,128)(2,1)S(1)}, bf16[256,512]{1,0:T(8,128)(2,1)S(1)}, u32[]{:S(2)}, u32[]{:S(2)}) collective-permute-start(bf16[256,512]{1,0:T(8,128)(2,1)S(1)} %get-tuple-element.76.refs_1_), channel_id=1, source_target_pairs={{0,1},{1,0},{2,3},{3,2},{4,5},{5,4},{6,7},{7,6},{8,9},{9,8},{10,11... | collective-permute-start | bytes 786440 | tf_op jit(solution)/shard_map/ppermute | solution.py:514
  95.0 3.3 %copy-start.7 = (bf16[256,512]{1,0:T(8,128)(2,1)}, bf16[256,512]{1,0:T(8,128)(2,1)S(1)}, u32[]{:S(2)}) copy-start(bf16[256,512]{1,0:T(8,128)(2,1)S(1)} %collective-permute-done.20.refs_3_) | copy-start | bytes 786436
  95.0 3.3 %collective-permute-start.21 = (bf16[256,512]{1,0:T(8,128)(2,1)S(1)}, bf16[256,512]{1,0:T(8,128)(2,1)S(1)}, u32[]{:S(2)}, u32[]{:S(2)}) collective-permute-start(bf16[256,512]{1,0:T(8,128)(2,1)S(1)} %collective-permute-done.20.refs_3_), channel_id=1, source_target_pairs={{0,1},{1,0},{2,3},{3,2},{4,5},{5,4},{6,7},{7,6},{8,9},{9,8},{10,11... | collective-permute-start | bytes 786440 | tf_op jit(solution)/shard_map/ppermute | solution.py:514
  96.7 1.5 %copy-start.8 = (bf16[256,512]{1,0:T(8,128)(2,1)}, bf16[256,512]{1,0:T(8,128)(2,1)S(1)}, u32[]{:S(2)}) copy-start(bf16[256,512]{1,0:T(8,128)(2,1)S(1)} %collective-permute-done.12.refs_2_) | copy-start | bytes 786436
  96.7 20.7 %collective-permute-start.22 = (bf16[128,2560]{1,0:T(8,128)(2,1)S(1)}, bf16[128,2560]{1,0:T(8,128)(2,1)S(1)}, u32[]{:S(2)}, u32[]{:S(2)}) collective-permute-start(bf16[128,2560]{1,0:T(8,128)(2,1)S(1)} %join.1), channel_id=1, source_target_pairs={{0,2},{1,3},{2,0},{3,1},{4,6},{5,7},{6,4},{7,5},{8,10},{9,11},{10,... | collective-permute-start | bytes 1966088 | tf_op jit(solution)/shard_map/ppermute | solution.py:517
  98.2 0.7 copy-start.9
  117.3 2.2 %copy-start.1 = (f32[3,2560]{1,0:T(4,128)S(1)}, f32[3,2560]{1,0:T(4,128)}, u32[]{:S(2)}) copy-start(f32[3,2560]{1,0:T(4,128)} %pad_maximum_fusion.1.refs_5_.refs_2_) | copy-start | bytes 92164
  117.4 1.7 %collective-permute-start.23 = (bf16[64,2560]{1,0:T(8,128)(2,1)S(1)}, bf16[64,2560]{1,0:T(8,128)(2,1)S(1)}, u32[]{:S(2)}, u32[]{:S(2)}) collective-permute-start(bf16[64,2560]{1,0:T(8,128)(2,1)S(1)} %get-tuple-element.85), channel_id=1, source_target_pairs={{0,1},{1,0},{2,3},{3,2},{4,5},{5,4},{6,7},{7,6},{8,9},{9,8},{10,11... | collective-permute-start | bytes 983048 | tf_op jit(solution)/shard_map/ppermute | solution.py:514
  117.4 2.1 %collective-permute-start.24 = (bf16[64,2560]{1,0:T(8,128)(2,1)S(1)}, bf16[64,2560]{1,0:T(8,128)(2,1)S(1)}, u32[]{:S(2)}, u32[]{:S(2)}) collective-permute-start(bf16[64,2560]{1,0:T(8,128)(2,1)S(1)} %get-tuple-element.86), channel_id=1, source_target_pairs={{0,1},{1,0},{2,3},{3,2},{4,5},{5,4},{6,7},{7,6},{8,9},{9,8},{10,11... | collective-permute-start | bytes 983048 | tf_op jit(solution)/shard_map/ppermute | solution.py:514

commit v3 on v2

--- a/solution.py
+++ b/solution.py
@@ -169,7 +169,7 @@
             for copy in copies_of(at):
                 copy.wait()
 
-            @pl.loop(0, row_count // step)
+            @pl.loop(0, row_count // step, unroll=2 if parts else 1)
             def _(turn):
                 rows = pl.ds(pl.multiple_of(turn * step, step), step)
                 for head in range(heads):

time: 122 us -> 122 us (level)
  transfers between devices with their start and end apart: 25 -> 25, of which waited for: 14 -> 13; matrix products, arithmetic and copies ran while one was open for 4% -> 4% of each run, Pallas kernels for 45% -> 44%
where the time goes in v3:
time: 122 us; the launch traced here: 121 us
  Pallas kernels  54.5 us (45%)
  starting transfers between devices  33.9 us (28%)
  waiting for transfers between devices  24.2 us (20%)
  local copies, waits for them, and re-layouts  5.88 us (5%)
  other arithmetic  2.17 us (2%)
    pallas_call x2, Pallas kernels, feed_rows(): pl.pallas_call(functools.partial(feed_kernel, pieces, group, planes), in_...  36.4 us
    ppermute x11, starting transfers between devices, move(): return lax.ppermute(values_in, 'req', pairs)  26.4 us
    pallas_call x5, Pallas kernels, attention_call(): pl.pallas_call(kernel, in_specs=in_specs, out_specs=[VMEM] * len(out_shap...  14.8 us
    ppermute x11, waiting for transfers between devices, move(): return lax.ppermute(values_in, 'req', pairs)  12.4 us
    ppermute x4, waiting for transfers between devices, plane_shift(): lax.ppermute(values_in, 'tok', [(at, (at + CORES * shift) % tok_count) fo...  8 us
    ppermute x4, starting transfers between devices, plane_shift(): lax.ppermute(values_in, 'tok', [(at, (at + CORES * shift) % tok_count) fo...  5.56 us
    ppermute x10, waiting for transfers between devices, other_core(): lax.ppermute(values_in, 'tok', [(at, at ^ 1) for at in range(tok_count)])  3.82 us
  transfers between devices with their start and end apart: 25, of which 13 were waited for; matrix products, arithmetic and copies ran while one was open for 4% of the time, Pallas kernels for 44%

profile of v3, /device:TPU:0, one launch (start us, length us, event | category | flops | bytes accessed | tf_op | source)
XLA Modules:
  0.0 120.9 jit_solution(16223644955624968826)
XLA Ops:
  0.0 1.1 constant_dynamic-slice_fusion.1
  1.1 0.8 pad_maximum_fusion.refs_4_
  1.9 3.0 %collective-permute-start = (bf16[512,2560]{1,0:T(8,128)(2,1)}, bf16[512,2560]{1,0:T(8,128)(2,1)S(1)}, u32[]{:S(2)}, u32[]{:S(2)}) collective-permute-start(bf16[512,2560]{1,0:T(8,128)(2,1)} %refs_12_.3), channel_id=1, source_target_pairs={{0,2},{1,3},{2,0},{3,1},{4,6},{5,7},{6,4},{7,5},{8,10},{9,11},{10,... | collective-permute-start | bytes 7864328 | tf_op jit(solution)/shard_map/ppermute | solution.py:517
  4.9 1.5 %collective-permute-start.3 = (bf16[512,512]{1,0:T(8,128)(2,1)}, bf16[512,512]{1,0:T(8,128)(2,1)}, u32[]{:S(2)}, u32[]{:S(2)}) collective-permute-start(bf16[512,512]{1,0:T(8,128)(2,1)} %pad_maximum_fusion.refs_4_), channel_id=1, source_target_pairs={{0,4},{4,0},{8,12},{12,8},{16,20},{20,16},{24,28},{28,24},{1,5},{5... | collective-permute-start | bytes 1572872 | tf_op jit(solution)/shard_map/ppermute | solution.py:511
  6.4 1.3 %collective-permute-start.2 = (bf16[512,512]{1,0:T(8,128)(2,1)}, bf16[512,512]{1,0:T(8,128)(2,1)S(1)}, u32[]{:S(2)}, u32[]{:S(2)}) collective-permute-start(bf16[512,512]{1,0:T(8,128)(2,1)} %pad_maximum_fusion.refs_4_), channel_id=1, source_target_pairs={{8,0},{12,4},{16,8},{20,12},{24,16},{28,20},{9,1},{13,5},{17,9},{2... | collective-permute-start | bytes 1572872 | tf_op jit(solution)/shard_map/ppermute | solution.py:511
  7.7 5.4 %collective-permute-start.1 = (bf16[512,512]{1,0:T(8,128)(2,1)}, bf16[512,512]{1,0:T(8,128)(2,1)}, u32[]{:S(2)}, u32[]{:S(2)}) collective-permute-start(bf16[512,512]{1,0:T(8,128)(2,1)} %pad_maximum_fusion.refs_4_), channel_id=1, source_target_pairs={{0,8},{4,12},{8,16},{12,20},{16,24},{20,28},{1,9},{5,13},{9,17},{1... | collective-permute-start | bytes 1572872 | tf_op jit(solution)/shard_map/ppermute | solution.py:511
  13.0 0.7 stack.33
  13.8 0.7 stack.34
  14.5 0.7 stack.35
  15.2 0.8 concatenate.6.refs_0_.numbers
  15.9 0.6 pad_maximum_fusion.1.refs_5_.refs_2_
  16.6 0.7 pad_maximum_fusion.2.refs_3_
  17.3 5.3 %attend_blocks.5 = (bf16[512,512]{1,0:T(8,128)(2,1)S(1)}, f32[2,512,128]{2,1,0:T(8,128)S(1)}, f32[2,512,128]{2,1,0:T(8,128)S(1)}, f32[512,512]{1,0:T(8,128)S(1)}) custom-call(s32[22]{0:T(128)S(1)} %concatenate.6.refs_0_.numbers, bf16[512,512]{1,0:T(8,128)(2,1)} %refs_1_.1, bf16[512,2048]{1,0:T(8,128)(2,1)} %refs_2_.1, ...), custom_call_target="tpu_custom_call" | custom-call | flops 1073741824 | bytes 4194304 | tf_op jit(solution)/shard_map/attend_blocks/pallas_call | solution.py:227
  22.8 0.7 collective-permute-start.4
  23.5 1.3 %collective-permute-start.5 = (bf16[512,512]{1,0:T(8,128)(2,1)S(1)}, bf16[512,512]{1,0:T(8,128)(2,1)S(1)}, u32[]{:S(2)}, u32[]{:S(2)}) collective-permute-start(bf16[512,512]{1,0:T(8,128)(2,1)S(1)} %collective-permute-done.2.refs_6_.lower_ref), channel_id=1, source_target_pairs={{16,8},{20,12},{8,0},{12,4},{17,9},{21,13},{9,1},{13,5},{18,10},{2... | collective-permute-start | bytes 1572872 | tf_op jit(solution)/shard_map/ppermute | solution.py:511
  24.8 1.1 pick.2
  25.9 0.6 collective-permute-start.6
  26.5 7.9 %collective-permute-start.7 = (bf16[512,512]{1,0:T(8,128)(2,1)}, bf16[512,512]{1,0:T(8,128)(2,1)S(1)}, u32[]{:S(2)}, u32[]{:S(2)}) collective-permute-start(bf16[512,512]{1,0:T(8,128)(2,1)} %collective-permute-done.3.refs_7_), channel_id=1, source_target_pairs={{0,8},{4,12},{24,16},{28,20},{1,9},{5,13},{25,17},{29,21},{2,10},{... | collective-permute-start | bytes 1572872 | tf_op jit(solution)/shard_map/ppermute | solution.py:511
  34.4 4.8 %attend_blocks.6 = (f32[2,512,128]{2,1,0:T(8,128)S(1)}, f32[2,512,128]{2,1,0:T(8,128)S(1)}, f32[512,512]{1,0:T(8,128)S(1)}) custom-call(s32[22]{0:T(128)S(1)} %concatenate.6.refs_0_.numbers, bf16[512,512]{1,0:T(8,128)(2,1)S(1)} %get-tuple-element.49.refs_1_, f32[2,512,128]{2,1,0:T(8,128)S(1)} %get-tuple-element.50.refs_2_, ...), custom_call_target="tpu_custom_call" | custom-call | flops 1073741824 | bytes 4194304 | tf_op jit(solution)/shard_map/attend_blocks/pallas_call | solution.py:227
  39.2 1.4 %collective-permute-done.5.refs_6_.lower_ref = bf16[512,512]{1,0:T(8,128)(2,1)S(1)} collective-permute-done((bf16[512,512]{1,0:T(8,128)(2,1)S(1)}, bf16[512,512]{1,0:T(8,128)(2,1)S(1)}, u32[]{:S(2)}, u32[]{:S(2)}) %collective-permute-start.5) | collective-permute-done | bytes 524320 | tf_op jit(solution)/shard_map/ppermute | solution.py:511
  40.6 0.6 pick.3
  41.2 0.6 collective-permute-start.9
  41.8 1.3 %collective-permute-start.8 = (bf16[512,512]{1,0:T(8,128)(2,1)S(1)}, bf16[512,512]{1,0:T(8,128)(2,1)S(1)}, u32[]{:S(2)}, u32[]{:S(2)}) collective-permute-start(bf16[512,512]{1,0:T(8,128)(2,1)S(1)} %pick.3), channel_id=1, source_target_pairs={{16,24},{20,28},{8,0},{12,4},{17,25},{21,29},{9,1},{13,5},{18,26},... | collective-permute-start | bytes 1572872 | tf_op jit(solution)/shard_map/ppermute | solution.py:511
  43.1 0.4 collective-permute-done.7.refs_8_
  43.5 0.8 attend_blocks.7
  44.4 7.9 %collective-permute-done.9.refs_6_ = bf16[512,512]{1,0:T(8,128)(2,1)S(1)} collective-permute-done((bf16[512,512]{1,0:T(8,128)(2,1)S(1)}, bf16[512,512]{1,0:T(8,128)(2,1)S(1)}, u32[]{:S(2)}, u32[]{:S(2)}) %collective-permute-start.9) | collective-permute-done | bytes 524320 | tf_op jit(solution)/shard_map/ppermute | solution.py:511
  52.3 1.3 %collective-permute-start.11 = (bf16[256,512]{1,0:T(8,128)(2,1)S(1)}, bf16[256,512]{1,0:T(8,128)(2,1)S(1)}, u32[]{:S(2)}, u32[]{:S(2)}) collective-permute-start(bf16[256,512]{1,0:T(8,128)(2,1)S(1)} %slice.8), channel_id=1, source_target_pairs={{16,24},{20,28},{8,0},{12,4},{17,25},{21,29},{9,1},{13,5},{18,26},... | collective-permute-start | bytes 786440 | tf_op jit(solution)/shard_map/ppermute | solution.py:511
  53.6 1.2 collective-permute-done.8.refs_5_
  54.8 4.6 %collective-permute-start.10 = (bf16[256,512]{1,0:T(8,128)(2,1)S(1)}, bf16[256,512]{1,0:T(8,128)(2,1)S(1)}, u32[]{:S(2)}, u32[]{:S(2)}) collective-permute-start(bf16[256,512]{1,0:T(8,128)(2,1)S(1)} %slice.6), channel_id=1, source_target_pairs={{0,4},{4,0},{24,28},{28,24},{1,5},{5,1},{25,29},{29,25},{2,6},{6,2... | collective-permute-start | bytes 786440 | tf_op jit(solution)/shard_map/ppermute | solution.py:511
  59.4 2.9 %attend_blocks.8 = (f32[2,512,128]{2,1,0:T(8,128)S(1)}, f32[2,512,128]{2,1,0:T(8,128)S(1)}, f32[512,512]{1,0:T(8,128)S(1)}) custom-call(s32[22]{0:T(128)S(1)} %concatenate.6.refs_0_.numbers, bf16[512,512]{1,0:T(8,128)(2,1)S(1)} %get-tuple-element.49.refs_1_, f32[2,512,128]{2,1,0:T(8,128)S(1)} %get-tuple-element.58.refs_2_, ...), custom_call_target="tpu_custom_call" | custom-call | flops 1073741824 | bytes 4194304 | tf_op jit(solution)/shard_map/attend_blocks/pallas_call | solution.py:227
  62.4 1.3 %collective-permute-done.10.refs_5_ = bf16[256,512]{1,0:T(8,128)(2,1)S(1)} collective-permute-done((bf16[256,512]{1,0:T(8,128)(2,1)S(1)}, bf16[256,512]{1,0:T(8,128)(2,1)S(1)}, u32[]{:S(2)}, u32[]{:S(2)}) %collective-permute-start.10) | collective-permute-done | bytes 262176 | tf_op jit(solution)/shard_map/ppermute | solution.py:511
  63.7 0.9 attend_blocks.9
  64.8 0.6 collective-permute-start.14
  65.5 8.0 %collective-permute-done.14.refs_3_ = bf16[256,512]{1,0:T(8,128)(2,1)S(1)} collective-permute-done((bf16[256,512]{1,0:T(8,128)(2,1)S(1)}, bf16[256,512]{1,0:T(8,128)(2,1)S(1)}, u32[]{:S(2)}, u32[]{:S(2)}) %collective-permute-start.14) | collective-permute-done | bytes 262176 | tf_op jit(solution)/shard_map/ppermute | solution.py:517
  73.5 0.5 collective-permute-start.20
  74.0 1.0 collective-permute-done.15.refs_4_
  75.0 0.5 copy-done.6
  75.6 0.6 copy-done.12
  76.2 18.1 %feed_rows.2 = (f32[128,2560]{1,0:T(8,128)S(1)}, bf16[64,2560]{1,0:T(8,128)(2,1)S(1)}, bf16[64,2560]{1,0:T(8,128)(2,1)S(1)}) custom-call(s32[22]{0:T(128)} %copy-done.4, bf16[256,512]{1,0:T(8,128)(2,1)} %copy-done.3, bf16[256,512]{1,0:T(8,128)(2,1)} %copy-done.11, bf16[256,512]{1,0:T(8,128)(2,1)} %copy-done.10, bf16[256,512]{1,0:T(8,128)(2,1)} %copy-done.12, ...), custom_call_target="tpu_custom_call" | custom-call | flops 12750684160 | bytes 16777216 | tf_op jit(solution)/shard_map/feed_rows/pallas_call | solution.py:389
  95.3 0.6 collective-permute-done.18.refs_0_
  95.9 0.5 collective-permute-done.19.refs_1_
  96.8 1.5 %collective-permute-start.22 = (bf16[128,2560]{1,0:T(8,128)(2,1)S(1)}, bf16[128,2560]{1,0:T(8,128)(2,1)S(1)}, u32[]{:S(2)}, u32[]{:S(2)}) collective-permute-start(bf16[128,2560]{1,0:T(8,128)(2,1)S(1)} %join.1), channel_id=1, source_target_pairs={{0,2},{1,3},{2,0},{3,1},{4,6},{5,7},{6,4},{7,5},{8,10},{9,11},{10,... | collective-permute-start | bytes 1966088 | tf_op jit(solution)/shard_map/ppermute | solution.py:517
  98.3 0.7 copy-done.9
  99.0 18.4 %feed_rows.3 = (f32[128,2560]{1,0:T(8,128)S(1)}, bf16[64,2560]{1,0:T(8,128)(2,1)S(1)}, bf16[64,2560]{1,0:T(8,128)(2,1)S(1)}, f32[128,2560]{1,0:T(8,128)S(1)}) custom-call(s32[22]{0:T(128)} %copy-done.4, bf16[256,512]{1,0:T(8,128)(2,1)} %copy-done.2, bf16[256,512]{1,0:T(8,128)(2,1)} %copy-done.8, bf16[256,512]{1,0:T(8,128)(2,1)} %copy-done.7, ...), custom_call_target="tpu_custom_call" | custom-call | flops 12750684160 | bytes 16777216 | tf_op jit(solution)/shard_map/feed_rows/pallas_call | solution.py:389
  117.5 0.5 collective-permute-start.24
  118.1 1.0 collective-permute-done.23.refs_0_
  119.1 0.5 collective-permute-done.24.refs_1_
  119.6 1.3 %finish.1 = bf16[128,2560]{1,0:T(8,128)(2,1)} custom-call(f32[128,2560]{1,0:T(8,128)S(1)} %get-tuple-element.79.mixed_ref, f32[128,2560]{1,0:T(8,128)S(1)} %fold.1.total_ref, bf16[64,2560]{1,0:T(8,128)(2,1)S(1)} %collective-permute-done.23.refs_0_, bf16[64,2560]{1,0:T(8,128)(2,1)S(1)} %collective-permute-done.24.refs_1_, f32[3,2560]{1,0:T(4,128)S(1)} %copy-done.1), custom_call_target="tpu_custom_call" | custom-call | tf_op jit(solution)/shard_map/finish/pallas_call | solution.py:463
  (50 shorter events, 2.3 us)
Async XLA Ops:
  1.9 62.8 %collective-permute-start = (bf16[512,2560]{1,0:T(8,128)(2,1)}, bf16[512,2560]{1,0:T(8,128)(2,1)S(1)}, u32[]{:S(2)}, u32[]{:S(2)}) collective-permute-start(bf16[512,2560]{1,0:T(8,128)(2,1)} %refs_12_.3), channel_id=1, source_target_pairs={{0,2},{1,3},{2,0},{3,1},{4,6},{5,7},{6,4},{7,5},{8,10},{9,11},{10,... | collective-permute-start | bytes 7864328 | tf_op jit(solution)/shard_map/ppermute | solution.py:517
  4.9 21.7 %collective-permute-start.3 = (bf16[512,512]{1,0:T(8,128)(2,1)}, bf16[512,512]{1,0:T(8,128)(2,1)}, u32[]{:S(2)}, u32[]{:S(2)}) collective-permute-start(bf16[512,512]{1,0:T(8,128)(2,1)} %pad_maximum_fusion.refs_4_), channel_id=1, source_target_pairs={{0,4},{4,0},{8,12},{12,8},{16,20},{20,16},{24,28},{28,24},{1,5},{5... | collective-permute-start | bytes 1572872 | tf_op jit(solution)/shard_map/ppermute | solution.py:511
  6.4 16.3 %collective-permute-start.2 = (bf16[512,512]{1,0:T(8,128)(2,1)}, bf16[512,512]{1,0:T(8,128)(2,1)S(1)}, u32[]{:S(2)}, u32[]{:S(2)}) collective-permute-start(bf16[512,512]{1,0:T(8,128)(2,1)} %pad_maximum_fusion.refs_4_), channel_id=1, source_target_pairs={{8,0},{12,4},{16,8},{20,12},{24,16},{28,20},{9,1},{13,5},{17,9},{2... | collective-permute-start | bytes 1572872 | tf_op jit(solution)/shard_map/ppermute | solution.py:511
  7.7 15.2 %collective-permute-start.1 = (bf16[512,512]{1,0:T(8,128)(2,1)}, bf16[512,512]{1,0:T(8,128)(2,1)}, u32[]{:S(2)}, u32[]{:S(2)}) collective-permute-start(bf16[512,512]{1,0:T(8,128)(2,1)} %pad_maximum_fusion.refs_4_), channel_id=1, source_target_pairs={{0,8},{4,12},{8,16},{12,20},{16,24},{20,28},{1,9},{5,13},{9,17},{1... | collective-permute-start | bytes 1572872 | tf_op jit(solution)/shard_map/ppermute | solution.py:511
  15.9 47.8 %copy-start.4 = (s32[22]{0:T(128)}, s32[22]{0:T(128)S(1)}, u32[]{:S(2)}) copy-start(s32[22]{0:T(128)S(1)} %concatenate.6.refs_0_.numbers) | copy-start | bytes 268
  22.8 16.4 %collective-permute-start.4 = (bf16[512,512]{1,0:T(8,128)(2,1)}, bf16[512,512]{1,0:T(8,128)(2,1)S(1)}, u32[]{:S(2)}, u32[]{:S(2)}) collective-permute-start(bf16[512,512]{1,0:T(8,128)(2,1)} %collective-permute-done.1.refs_5_.upper_ref), channel_id=1, source_target_pairs={{8,16},{12,20},{16,24},{20,28},{9,17},{13,21},{17,25},{21,29},{10,... | collective-permute-start | bytes 1572872 | tf_op jit(solution)/shard_map/ppermute | solution.py:511
  23.5 17.1 %collective-permute-start.5 = (bf16[512,512]{1,0:T(8,128)(2,1)S(1)}, bf16[512,512]{1,0:T(8,128)(2,1)S(1)}, u32[]{:S(2)}, u32[]{:S(2)}) collective-permute-start(bf16[512,512]{1,0:T(8,128)(2,1)S(1)} %collective-permute-done.2.refs_6_.lower_ref), channel_id=1, source_target_pairs={{16,8},{20,12},{8,0},{12,4},{17,9},{21,13},{9,1},{13,5},{18,10},{2... | collective-permute-start | bytes 1572872 | tf_op jit(solution)/shard_map/ppermute | solution.py:511
  25.9 17.6 %collective-permute-start.6 = (bf16[512,512]{1,0:T(8,128)(2,1)S(1)}, bf16[512,512]{1,0:T(8,128)(2,1)S(1)}, u32[]{:S(2)}, u32[]{:S(2)}) collective-permute-start(bf16[512,512]{1,0:T(8,128)(2,1)S(1)} %pick.2), channel_id=1, source_target_pairs={{0,4},{4,0},{8,12},{12,8},{16,20},{20,16},{24,28},{28,24},{1,5},{5... | collective-permute-start | bytes 1572872 | tf_op jit(solution)/shard_map/ppermute | solution.py:511
  26.5 17.0 %collective-permute-start.7 = (bf16[512,512]{1,0:T(8,128)(2,1)}, bf16[512,512]{1,0:T(8,128)(2,1)S(1)}, u32[]{:S(2)}, u32[]{:S(2)}) collective-permute-start(bf16[512,512]{1,0:T(8,128)(2,1)} %collective-permute-done.3.refs_7_), channel_id=1, source_target_pairs={{0,8},{4,12},{24,16},{28,20},{1,9},{5,13},{25,17},{29,21},{2,10},{... | collective-permute-start | bytes 1572872 | tf_op jit(solution)/shard_map/ppermute | solution.py:511
  34.4 25.0 %copy-start.5 = (bf16[512,2560]{1,0:T(8,128)(2,1)S(1)}, bf16[512,2560]{1,0:T(8,128)(2,1)}, u32[]{:S(2)}) copy-start(bf16[512,2560]{1,0:T(8,128)(2,1)} %refs_12_.3) | copy-start | bytes 7864324
  41.2 11.0 %collective-permute-start.9 = (bf16[512,512]{1,0:T(8,128)(2,1)S(1)}, bf16[512,512]{1,0:T(8,128)(2,1)S(1)}, u32[]{:S(2)}, u32[]{:S(2)}) collective-permute-start(bf16[512,512]{1,0:T(8,128)(2,1)S(1)} %pick.3), channel_id=1, source_target_pairs={{0,4},{4,0},{8,12},{12,8},{16,20},{20,16},{24,28},{28,24},{1,5},{5... | collective-permute-start | bytes 1572872 | tf_op jit(solution)/shard_map/ppermute | solution.py:511
  41.8 12.9 %collective-permute-start.8 = (bf16[512,512]{1,0:T(8,128)(2,1)S(1)}, bf16[512,512]{1,0:T(8,128)(2,1)S(1)}, u32[]{:S(2)}, u32[]{:S(2)}) collective-permute-start(bf16[512,512]{1,0:T(8,128)(2,1)S(1)} %pick.3), channel_id=1, source_target_pairs={{16,24},{20,28},{8,0},{12,4},{17,25},{21,29},{9,1},{13,5},{18,26},... | collective-permute-start | bytes 1572872 | tf_op jit(solution)/shard_map/ppermute | solution.py:511
  43.5 32.6 %copy-start = (bf16[2560,2560]{1,0:T(8,128)(2,1)S(1)}, bf16[2560,2560]{1,0:T(8,128)(2,1)}, u32[]{:S(2)}) copy-start(bf16[2560,2560]{1,0:T(8,128)(2,1)} %refs_6_.3) | copy-start | bytes 39321604
  52.3 10.1 %collective-permute-start.11 = (bf16[256,512]{1,0:T(8,128)(2,1)S(1)}, bf16[256,512]{1,0:T(8,128)(2,1)S(1)}, u32[]{:S(2)}, u32[]{:S(2)}) collective-permute-start(bf16[256,512]{1,0:T(8,128)(2,1)S(1)} %slice.8), channel_id=1, source_target_pairs={{16,24},{20,28},{8,0},{12,4},{17,25},{21,29},{9,1},{13,5},{18,26},... | collective-permute-start | bytes 786440 | tf_op jit(solution)/shard_map/ppermute | solution.py:511
  54.8 8.9 %collective-permute-start.10 = (bf16[256,512]{1,0:T(8,128)(2,1)S(1)}, bf16[256,512]{1,0:T(8,128)(2,1)S(1)}, u32[]{:S(2)}, u32[]{:S(2)}) collective-permute-start(bf16[256,512]{1,0:T(8,128)(2,1)S(1)} %slice.6), channel_id=1, source_target_pairs={{0,4},{4,0},{24,28},{28,24},{1,5},{5,1},{25,29},{29,25},{2,6},{6,2... | collective-permute-start | bytes 786440 | tf_op jit(solution)/shard_map/ppermute | solution.py:511
  59.4 14.6 %collective-permute-start.17 = (bf16[512,2560]{1,0:T(8,128)(2,1)S(1)}, bf16[512,2560]{1,0:T(8,128)(2,1)S(1)}, u32[]{:S(2)}, u32[]{:S(2)}) collective-permute-start(bf16[512,2560]{1,0:T(8,128)(2,1)S(1)} %copy-done.5), channel_id=1, source_target_pairs={{0,1},{1,0},{2,3},{3,2},{4,5},{5,4},{6,7},{7,6},{8,9},{9,8},{10,11... | collective-permute-start | bytes 7864328 | tf_op jit(solution)/shard_map/ppermute | solution.py:514
  64.6 10.8 %copy-start.3 = (bf16[256,512]{1,0:T(8,128)(2,1)}, bf16[256,512]{1,0:T(8,128)(2,1)S(1)}, u32[]{:S(2)}) copy-start(bf16[256,512]{1,0:T(8,128)(2,1)S(1)} %get-tuple-element.78.refs_1_) | copy-start | bytes 786436
  64.7 30.1 %copy-start.2 = (bf16[256,512]{1,0:T(8,128)(2,1)}, bf16[256,512]{1,0:T(8,128)(2,1)S(1)}, u32[]{:S(2)}) copy-start(bf16[256,512]{1,0:T(8,128)(2,1)S(1)} %get-tuple-element.76.refs_1_) | copy-start | bytes 786436
  64.7 10.8 %collective-permute-start.16 = (bf16[512,2560]{1,0:T(8,128)(2,1)S(1)}, bf16[512,2560]{1,0:T(8,128)(2,1)S(1)}, u32[]{:S(2)}, u32[]{:S(2)}) collective-permute-start(bf16[512,2560]{1,0:T(8,128)(2,1)S(1)} %collective-permute-done.refs_7_), channel_id=1, source_target_pairs={{0,1},{1,0},{2,3},{3,2},{4,5},{5,4},{6,7},{7,6},{8,9},{9,8},{10,11... | collective-permute-start | bytes 7864328 | tf_op jit(solution)/shard_map/ppermute | solution.py:514
  64.8 8.7 %collective-permute-start.14 = (bf16[256,512]{1,0:T(8,128)(2,1)S(1)}, bf16[256,512]{1,0:T(8,128)(2,1)S(1)}, u32[]{:S(2)}, u32[]{:S(2)}) collective-permute-start(bf16[256,512]{1,0:T(8,128)(2,1)S(1)} %get-tuple-element.76.refs_1_), channel_id=1, source_target_pairs={{0,2},{1,3},{2,0},{3,1},{4,6},{5,7},{6,4},{7,5},{8,10},{9,11},{10,... | collective-permute-start | bytes 786440 | tf_op jit(solution)/shard_map/ppermute | solution.py:517
  65.3 8.7 %collective-permute-start.13 = (bf16[256,512]{1,0:T(8,128)(2,1)S(1)}, bf16[256,512]{1,0:T(8,128)(2,1)S(1)}, u32[]{:S(2)}, u32[]{:S(2)}) collective-permute-start(bf16[256,512]{1,0:T(8,128)(2,1)S(1)} %get-tuple-element.78.refs_1_), channel_id=1, source_target_pairs={{0,1},{1,0},{2,3},{3,2},{4,5},{5,4},{6,7},{7,6},{8,9},{9,8},{10,11... | collective-permute-start | bytes 786440 | tf_op jit(solution)/shard_map/ppermute | solution.py:514
  73.5 2.0 %copy-start.10 = (bf16[256,512]{1,0:T(8,128)(2,1)}, bf16[256,512]{1,0:T(8,128)(2,1)S(1)}, u32[]{:S(2)}) copy-start(bf16[256,512]{1,0:T(8,128)(2,1)S(1)} %collective-permute-done.14.refs_3_) | copy-start | bytes 786436
  73.5 1.5 %collective-permute-start.15 = (bf16[256,512]{1,0:T(8,128)(2,1)S(1)}, bf16[256,512]{1,0:T(8,128)(2,1)S(1)}, u32[]{:S(2)}, u32[]{:S(2)}) collective-permute-start(bf16[256,512]{1,0:T(8,128)(2,1)S(1)} %collective-permute-done.14.refs_3_), channel_id=1, source_target_pairs={{0,1},{1,0},{2,3},{3,2},{4,5},{5,4},{6,7},{7,6},{8,9},{9,8},{10,11... | collective-permute-start | bytes 786440 | tf_op jit(solution)/shard_map/ppermute | solution.py:514
  73.5 21.5 %collective-permute-start.20 = (bf16[256,512]{1,0:T(8,128)(2,1)S(1)}, bf16[256,512]{1,0:T(8,128)(2,1)S(1)}, u32[]{:S(2)}, u32[]{:S(2)}) collective-permute-start(bf16[256,512]{1,0:T(8,128)(2,1)S(1)} %get-tuple-element.78.refs_1_), channel_id=1, source_target_pairs={{0,2},{1,3},{2,0},{3,1},{4,6},{5,7},{6,4},{7,5},{8,10},{9,11},{10,... | collective-permute-start | bytes 786440 | tf_op jit(solution)/shard_map/ppermute | solution.py:517
  74.0 1.5 %copy-start.6 = (bf16[512,2560]{1,0:T(8,128)(2,1)}, bf16[512,2560]{1,0:T(8,128)(2,1)S(1)}, u32[]{:S(2)}) copy-start(bf16[512,2560]{1,0:T(8,128)(2,1)S(1)} %collective-permute-done.17.refs_13_) | copy-start | bytes 7864324
  74.0 1.6 %copy-start.11 = (bf16[256,512]{1,0:T(8,128)(2,1)}, bf16[256,512]{1,0:T(8,128)(2,1)S(1)}, u32[]{:S(2)}) copy-start(bf16[256,512]{1,0:T(8,128)(2,1)S(1)} %collective-permute-done.13.refs_2_) | copy-start | bytes 786436
  75.5 0.7 copy-start.12
  94.2 1.7 %collective-permute-start.18 = (bf16[64,2560]{1,0:T(8,128)(2,1)S(1)}, bf16[64,2560]{1,0:T(8,128)(2,1)S(1)}, u32[]{:S(2)}, u32[]{:S(2)}) collective-permute-start(bf16[64,2560]{1,0:T(8,128)(2,1)S(1)} %get-tuple-element.74), channel_id=1, source_target_pairs={{0,1},{1,0},{2,3},{3,2},{4,5},{5,4},{6,7},{7,6},{8,9},{9,8},{10,11... | collective-permute-start | bytes 983048 | tf_op jit(solution)/shard_map/ppermute | solution.py:514
  94.5 1.9 %collective-permute-start.19 = (bf16[64,2560]{1,0:T(8,128)(2,1)S(1)}, bf16[64,2560]{1,0:T(8,128)(2,1)S(1)}, u32[]{:S(2)}, u32[]{:S(2)}) collective-permute-start(bf16[64,2560]{1,0:T(8,128)(2,1)S(1)} %get-tuple-element.75), channel_id=1, source_target_pairs={{0,1},{1,0},{2,3},{3,2},{4,5},{5,4},{6,7},{7,6},{8,9},{9,8},{10,11... | collective-permute-start | bytes 983048 | tf_op jit(solution)/shard_map/ppermute | solution.py:514
  94.8 2.0 %collective-permute-start.12 = (bf16[256,512]{1,0:T(8,128)(2,1)S(1)}, bf16[256,512]{1,0:T(8,128)(2,1)S(1)}, u32[]{:S(2)}, u32[]{:S(2)}) collective-permute-start(bf16[256,512]{1,0:T(8,128)(2,1)S(1)} %get-tuple-element.76.refs_1_), channel_id=1, source_target_pairs={{0,1},{1,0},{2,3},{3,2},{4,5},{5,4},{6,7},{7,6},{8,9},{9,8},{10,11... | collective-permute-start | bytes 786440 | tf_op jit(solution)/shard_map/ppermute | solution.py:514
  95.0 3.3 %copy-start.7 = (bf16[256,512]{1,0:T(8,128)(2,1)}, bf16[256,512]{1,0:T(8,128)(2,1)S(1)}, u32[]{:S(2)}) copy-start(bf16[256,512]{1,0:T(8,128)(2,1)S(1)} %collective-permute-done.20.refs_3_) | copy-start | bytes 786436
  95.0 3.3 %collective-permute-start.21 = (bf16[256,512]{1,0:T(8,128)(2,1)S(1)}, bf16[256,512]{1,0:T(8,128)(2,1)S(1)}, u32[]{:S(2)}, u32[]{:S(2)}) collective-permute-start(bf16[256,512]{1,0:T(8,128)(2,1)S(1)} %collective-permute-done.20.refs_3_), channel_id=1, source_target_pairs={{0,1},{1,0},{2,3},{3,2},{4,5},{5,4},{6,7},{7,6},{8,9},{9,8},{10,11... | collective-permute-start | bytes 786440 | tf_op jit(solution)/shard_map/ppermute | solution.py:514
  96.8 1.5 %copy-start.8 = (bf16[256,512]{1,0:T(8,128)(2,1)}, bf16[256,512]{1,0:T(8,128)(2,1)S(1)}, u32[]{:S(2)}) copy-start(bf16[256,512]{1,0:T(8,128)(2,1)S(1)} %collective-permute-done.12.refs_2_) | copy-start | bytes 786436
  96.8 20.7 %collective-permute-start.22 = (bf16[128,2560]{1,0:T(8,128)(2,1)S(1)}, bf16[128,2560]{1,0:T(8,128)(2,1)S(1)}, u32[]{:S(2)}, u32[]{:S(2)}) collective-permute-start(bf16[128,2560]{1,0:T(8,128)(2,1)S(1)} %join.1), channel_id=1, source_target_pairs={{0,2},{1,3},{2,0},{3,1},{4,6},{5,7},{6,4},{7,5},{8,10},{9,11},{10,... | collective-permute-start | bytes 1966088 | tf_op jit(solution)/shard_map/ppermute | solution.py:517
  98.3 0.7 copy-start.9
  117.4 2.2 %copy-start.1 = (f32[3,2560]{1,0:T(4,128)S(1)}, f32[3,2560]{1,0:T(4,128)}, u32[]{:S(2)}) copy-start(f32[3,2560]{1,0:T(4,128)} %pad_maximum_fusion.1.refs_5_.refs_2_) | copy-start | bytes 92164
  117.4 1.7 %collective-permute-start.23 = (bf16[64,2560]{1,0:T(8,128)(2,1)S(1)}, bf16[64,2560]{1,0:T(8,128)(2,1)S(1)}, u32[]{:S(2)}, u32[]{:S(2)}) collective-permute-start(bf16[64,2560]{1,0:T(8,128)(2,1)S(1)} %get-tuple-element.85), channel_id=1, source_target_pairs={{0,1},{1,0},{2,3},{3,2},{4,5},{5,4},{6,7},{7,6},{8,9},{9,8},{10,11... | collective-permute-start | bytes 983048 | tf_op jit(solution)/shard_map/ppermute | solution.py:514
  117.5 2.1 %collective-permute-start.24 = (bf16[64,2560]{1,0:T(8,128)(2,1)S(1)}, bf16[64,2560]{1,0:T(8,128)(2,1)S(1)}, u32[]{:S(2)}, u32[]{:S(2)}) collective-permute-start(bf16[64,2560]{1,0:T(8,128)(2,1)S(1)} %get-tuple-element.86), channel_id=1, source_target_pairs={{0,1},{1,0},{2,3},{3,2},{4,5},{5,4},{6,7},{7,6},{8,9},{9,8},{10,11... | collective-permute-start | bytes 983048 | tf_op jit(solution)/shard_map/ppermute | solution.py:514
